TPU v7x, 512 devices: a whole 4x4x16 slice. The times are simulated.
512 devices in a mesh: dap: 32 (over z, x_lo), pair: 16 (over y, x_hi, core).
Axes of the slice: x: 4 (x_hi: 2, x_lo: 2; x = x_hi * 2 + x_lo), y: 4, z: 16, core: 2. Of those that a mesh axis runs over, the one named last changes fastest.
Arguments:
- alignment_activity: bfloat16 [128, 512, 256], P('pair', 'dap'), may hold values from -6 to 6
- existing_strand_flags: int32 [128], replicated, may hold values from 0 to 1
- existing_position_flags: int32 [512], replicated, may hold values 0 or 1
- asking_vector_map: bfloat16 [256, 256], replicated, may hold values from -2.2 to 2.2
- lookup_address_map: bfloat16 [256, 256], replicated, may hold values from -2.2 to 2.2
- content_vector_map: bfloat16 [256, 256], replicated, may hold values from -0.375 to 0.375
- sigmoid_switch_map: bfloat16 [256, 256], replicated, may hold values from -0.375 to 0.375
- final_mixing_map: bfloat16 [256, 256], replicated, may hold values from -0.375 to 0.375
- final_offset_vector: float32 [256], replicated, may hold values from -3 to 3
- first_factor_map: bfloat16 [256, 32], replicated, may hold values from -0.375 to 0.375
- first_factor_offset: float32 [32], replicated, may hold values from -3 to 3
- second_factor_map: bfloat16 [256, 32], replicated, may hold values from -0.375 to 0.375
- second_factor_offset: float32 [32], replicated, may hold values from -3 to 3
- couple_mixing_map: bfloat16 [1024, 128], replicated, may hold values from -1 to 1
- couple_change_offset: float32 [128], replicated, may hold values from -3 to 3
Outputs:
- vertical_change: bfloat16 [128, 512, 256], P('pair', 'dap')
- pair_update: bfloat16 [512, 512, 128], P('dap', 'pair')
All inputs are finite; a program needn't handle non-finite values.
Results may differ from a plain program's by a relative error of at most 0.015.
Values may be sent and summed in bfloat16 or wider, within the bound.
A program may use at most 128 MiB of HBM per device.

v0:
```python
import jax
import jax.numpy as jnp
from jax import lax
from jax.sharding import PartitionSpec as P

C_Z = 128
HEADS = 8
HEAD_SIZE = 32
OUTER_FACTORS = 32


def standardize_entries(values):
    centered = values - jnp.mean(values, axis=-1, keepdims=True)
    spread = jnp.mean(centered * centered, axis=-1, keepdims=True)
    return centered * lax.rsqrt(spread + 1e-05)


def attend(
    items,
    asking_vector_map,
    lookup_address_map,
    content_vector_map,
    sigmoid_switch_map,
    final_mixing_map,
    final_offset_vector,
    key_bias,
):
    seqs, single, item_count, embedding_depth = items.shape
    flat_items = items.reshape(seqs * item_count, embedding_depth)
    inv_scale = HEAD_SIZE ** (-0.5)
    queries = (
        (jnp.dot(flat_items, asking_vector_map, preferred_element_type=jnp.float32) * inv_scale)
        .astype(jnp.bfloat16)
        .reshape(seqs, item_count, HEADS, HEAD_SIZE)
    )
    keys_all = (
        jnp.dot(flat_items, lookup_address_map, preferred_element_type=jnp.float32)
        .astype(jnp.bfloat16)
        .reshape(seqs, item_count, HEADS, HEAD_SIZE)
    )
    values_all = (
        jnp.dot(flat_items, content_vector_map, preferred_element_type=jnp.float32)
        .astype(jnp.bfloat16)
        .reshape(seqs, item_count, HEADS, HEAD_SIZE)
    )
    gates = jax.nn.sigmoid(
        jnp.dot(flat_items, sigmoid_switch_map, preferred_element_type=jnp.float32)
    ).reshape(seqs, item_count, HEADS, HEAD_SIZE)

    def one_head(head_index):
        query_head = lax.dynamic_index_in_dim(queries, head_index, 2, keepdims=False)
        key_head = lax.dynamic_index_in_dim(keys_all, head_index, 2, keepdims=False)
        value_head = lax.dynamic_index_in_dim(values_all, head_index, 2, keepdims=False)
        gate_head = lax.dynamic_index_in_dim(gates, head_index, 2, keepdims=False)
        scores = (
            jnp.einsum("skd,tkd->kst", query_head, key_head, preferred_element_type=jnp.float32)
            + key_bias[None, None, :]
        )
        scores = scores - jnp.max(scores, axis=-1, keepdims=True)
        weights = jnp.exp(scores)
        weights = (weights / jnp.sum(weights, axis=-1, keepdims=True)).astype(jnp.bfloat16)
        mixed = jnp.einsum("kst,tkd->skd", weights, value_head, preferred_element_type=jnp.float32)
        return (mixed * gate_head).astype(jnp.bfloat16)

    heads_out = lax.map(one_head, jnp.arange(HEADS, dtype=jnp.int32))
    joined = jnp.transpose(heads_out, (1, 2, 0, 3)).reshape(seqs * item_count, HEADS * HEAD_SIZE)
    update = (
        jnp.dot(joined, final_mixing_map, preferred_element_type=jnp.float32) + final_offset_vector
    )
    return update.astype(jnp.bfloat16).reshape(seqs, 1, item_count, embedding_depth)


def local(
    alignment_activity,
    existing_strand_flags,
    existing_position_flags,
    asking_vector_map,
    lookup_address_map,
    content_vector_map,
    sigmoid_switch_map,
    final_mixing_map,
    final_offset_vector,
    first_factor_map,
    first_factor_offset,
    second_factor_map,
    second_factor_offset,
    couple_mixing_map,
    couple_change_offset,
):
    shard_strands, shard_positions, embedding_depth = alignment_activity.shape
    groups = lax.axis_size("pair")
    standardized_source = standardize_entries(alignment_activity.astype(jnp.float32)).astype(
        jnp.bfloat16
    )
    keep = existing_strand_flags.astype(jnp.float32)
    key_bias = (keep - 1.0) * 1000000000.0
    kept = jnp.sum(keep)
    row_start = lax.axis_index("pair") * shard_strands
    residue_start = lax.axis_index("dap") * shard_positions
    keep_rows = lax.dynamic_slice_in_dim(keep, row_start, shard_strands)
    keep_residues = lax.dynamic_slice_in_dim(
        existing_position_flags.astype(jnp.float32), residue_start, shard_positions
    )
    both_masks = keep_rows[:, None, None] * keep_residues[None, :, None]
    unrolled_tensor = standardized_source.reshape(shard_strands * shard_positions, embedding_depth)
    left = (
        (
            jnp.dot(unrolled_tensor, first_factor_map, preferred_element_type=jnp.float32)
            + first_factor_offset
        ).reshape(shard_strands, shard_positions, OUTER_FACTORS)
        * both_masks
    ).astype(jnp.bfloat16)
    right = (
        (
            jnp.dot(unrolled_tensor, second_factor_map, preferred_element_type=jnp.float32)
            + second_factor_offset
        ).reshape(shard_strands, shard_positions, OUTER_FACTORS)
        * both_masks
    ).astype(jnp.bfloat16)
    blocks = standardized_source.reshape(
        shard_strands, groups, shard_positions // groups, embedding_depth
    )
    update = attend(
        lax.all_to_all(blocks, "pair", split_axis=1, concat_axis=0, tiled=True),
        asking_vector_map,
        lookup_address_map,
        content_vector_map,
        sigmoid_switch_map,
        final_mixing_map,
        final_offset_vector,
        key_bias,
    )
    columns = lax.all_to_all(update, "pair", split_axis=0, concat_axis=1, tiled=True)
    vertical_change = columns.reshape(shard_strands, shard_positions, embedding_depth)
    pair_matrix = couple_mixing_map.reshape(OUTER_FACTORS, OUTER_FACTORS * C_Z)
    right_all = lax.all_gather(right, "dap", axis=1, tiled=True)
    projected = (
        jnp.dot(
            left.reshape(shard_strands * shard_positions, OUTER_FACTORS),
            pair_matrix,
            preferred_element_type=jnp.float32,
        )
        .astype(jnp.bfloat16)
        .reshape(shard_strands, shard_positions, OUTER_FACTORS, C_Z)
    )
    summed = lax.psum_scatter(
        jnp.einsum(
            "sjc,sice->jie", right_all, projected, preferred_element_type=jnp.float32
        ).astype(jnp.bfloat16),
        "pair",
        scatter_dimension=0,
        tiled=True,
    ).astype(jnp.float32)
    total = jnp.transpose(summed, (1, 0, 2))
    pair_update = (total / kept + couple_change_offset).astype(jnp.bfloat16)
    return (vertical_change, pair_update)


def solution(mesh):
    return jax.shard_map(
        local,
        mesh=mesh,
        in_specs=(
            P("pair", "dap", None),
            P(),
            P(),
            P(),
            P(),
            P(),
            P(),
            P(),
            P(),
            P(),
            P(),
            P(),
            P(),
            P(),
            P(),
        ),
        out_specs=(P("pair", "dap", None), P("dap", "pair", None)),
        check_vma=False,
    )
```

profile of v0, /device:TPU:32, one launch (start us, length us, event | category | flops | bytes accessed | tf_op | source)
XLA Modules:
  0.0 191.2 jit_solution(6006425996117852435)
XLA Ops:
  7.2 0.7 convert_element_type.60
  8.1 0.7 convert_element_type.58
  9.1 0.9 convert_reduce_fusion
  10.0 1.0 fusion.28
  11.1 0.9 fusion.29
  12.0 1.1 reshape.145
  13.1 1.4 fusion.15
  14.5 0.2 copy.61
  14.8 0.1 copy.56
  15.1 71.9 %all_gather.3 = bf16[8,512,32]{2,1,0:T(8,128)(2,1)S(1)} all-gather(bf16[8,16,32]{2,1,0:T(8,128)(2,1)S(1)} %multiply_convert_fusion), channel_id=1, replica_groups=mesh['dap'=32,'pair'=16] {'dap'}, dimensions={1}, use_global_device_ids=true | all-gather | bytes 270336 | tf_op jit(solution)/shard_map/all_gather | solution.py:136
  86.9 2.7 %bitcast_convert_fusion = bf16[512,16,128]{2,0,1:T(8,128)(2,1)} fusion(bf16[8,512,32]{2,1,0:T(8,128)(2,1)S(1)} %all_gather.3, bf16[8,16,32,128]{3,2,1,0:T(8,128)(2,1)S(1)} %bitcast.112), kind=kOutput, calls=%fused_computation.20 | convolution fusion | flops 537919488 | bytes 3407872 | tf_op jit(solution)/shard_map/sjc,sice->jie/dot_general | solution.py:147
  89.7 0.8 copy-done.1
  90.6 0.7 copy.50
  91.3 7.2 %all-to-all-start = ((bf16[8,16,1,256]{3,0,2,1:T(8,128)(2,1)}), bf16[8,16,1,256]{3,0,2,1:T(8,128)(2,1)S(1)}, u32[]{:S(2)}, u32[]{:S(2)}) async-start(bf16[8,16,1,256]{3,0,2,1:T(8,128)(2,1)} %copy.50), calls=%async_computation | async-start | bytes 131072 | tf_op jit(solution)/shard_map/all_to_all | solution.py:124
  98.5 0.7 convert_reduce_fusion.1
  99.1 7.0 %all-to-all-done = bf16[8,16,1,256]{3,0,2,1:T(8,128)(2,1)S(1)} async-done(((bf16[8,16,1,256]{3,0,2,1:T(8,128)(2,1)}), bf16[8,16,1,256]{3,0,2,1:T(8,128)(2,1)S(1)}, u32[]{:S(2)}, u32[]{:S(2)}) %all-to-all-start) | async-done | bytes 65568 | tf_op jit(solution)/shard_map/all_to_all | solution.py:124
  106.1 0.2 fusion.18
  106.4 0.2 convolution_convert_fusion.2
  106.7 0.2 fusion.19
  107.1 0.2 convolution_convert_fusion.1
  107.4 23.7 %while.10 = (s32[]{:T(128)}, bf16[8,128,1,32]{1,3,2,0:T(8,128)(2,1)S(1)}, s32[8]{0:T(128)S(1)}, bf16[128,1,8,32]{0,3,2,1:T(8,128)(2,1)S(1)}, bf16[128,1,8,32]{0,...) while((s32[]{:T(128)}, ...), condition=%wide.region_5.6_spmd, body=%wide.region_2.5_spmd.sunk | while | flops 2219781 | bytes 251039 | solution.py:65
  107.4 0.6 dynamic_slice.52
  109.9 0.2 fusion.55
  110.2 0.1 fusion.57
  110.3 0.6 dynamic_slice.52
  112.9 0.2 fusion.55
  113.1 0.1 fusion.57
  113.3 0.6 dynamic_slice.52
  115.9 0.2 fusion.55
  116.3 0.6 dynamic_slice.52
  118.8 0.2 fusion.55
  119.1 0.1 fusion.57
  119.2 0.6 dynamic_slice.52
  121.8 0.2 fusion.55
  122.2 0.6 dynamic_slice.52
  124.7 0.2 fusion.55
  125.2 0.6 dynamic_slice.52
  127.7 0.2 fusion.55
  128.0 0.1 fusion.57
  128.1 0.6 dynamic_slice.52
  130.7 0.2 fusion.55
  131.1 0.2 fusion.21
  131.3 0.5 broadcast.75
  131.8 0.7 reduce.4
  132.5 10.6 %all_to_all.30 = bf16[16,2,1024]{2,1,0:T(2,128)(2,1)S(1)} all-to-all(bf16[16,2,1024]{2,1,0:T(2,128)(2,1)S(1)} %reshape.149), channel_id=1, replica_groups=mesh['dap'=32,'pair'=16] {'pair'}, dimensions={0} | all-to-all | bytes 131072 | tf_op jit(solution)/shard_map/all_to_all | solution.py:133
  143.3 0.6 copy.58
  143.9 38.2 %reduce-scatter.2.cloned.1.call-done = bf16[32,16,128]{2,0,1:T(8,128)(2,1)} async-done(((bf16[512,16,128]{2,0,1:T(8,128)(2,1)}), bf16[32,16,128]{2,0,1:T(8,128)(2,1)}) %reduce-scatter.2.cloned.1.call-update) | async-done | bytes 131088 | tf_op jit(solution)/shard_map/reduce_scatter | solution.py:146
  182.1 2.3 %fusion.30 = bf16[16,32,128]{2,1,0:T(8,128)(2,1)} fusion(bf16[32,16,128]{2,0,1:T(8,128)(2,1)} %reduce-scatter.2.cloned.1.call-done, f32[128]{0:T(128)S(1)} %copy-done.7, f32[]{:T(128)} %get-tuple-element.73), kind=kLoop, calls=%fused_computation.46 | loop fusion | flops 262144 | bytes 262660 | tf_op jit(solution)/shard_map/convert_element_type | solution.py:155
  (57 shorter events, 2.4 us)
Async XLA Ops:
  7.2 99.0 %copy-start = (bf16[256,256]{1,0:T(8,128)(2,1)S(1)}, bf16[256,256]{1,0:T(8,128)(2,1)}, u32[]{:S(2)}) copy-start(bf16[256,256]{1,0:T(8,128)(2,1)} %param.23) | copy-start | bytes 393220
  7.2 174.9 %reduce-scatter.2.cloned.1.call-start = ((), (), s32[]{:S(2)}) async-start(), calls=%async_computation.3 | async-start | bytes 2228224 | tf_op jit(solution)/shard_map/reduce_scatter | solution.py:146
  11.0 3.7 %copy-start.8 = (bf16[256,32]{0,1:T(8,128)(2,1)S(1)}, bf16[256,32]{0,1:T(8,128)(2,1)}, u32[]{:S(2)}) copy-start(bf16[256,32]{0,1:T(8,128)(2,1)} %param.28) | copy-start | bytes 49156
  11.0 3.7 %copy-start.9 = (f32[32]{0:T(128)S(1)}, f32[32]{0:T(128)}, u32[]{:S(2)}) copy-start(f32[32]{0:T(128)} %param.29) | copy-start | bytes 388
  89.7 0.8 copy-start.1
  89.7 8.8 %copy-start.10 = (s32[128]{0:T(128)S(1)}, s32[128]{0:T(128)}, u32[]{:S(2)}) copy-start(s32[128]{0:T(128)} %param.18) | copy-start | bytes 1540
  89.7 16.8 %copy-start.2 = (bf16[256,256]{1,0:T(8,128)(2,1)S(1)}, bf16[256,256]{1,0:T(8,128)(2,1)}, u32[]{:S(2)}) copy-start(bf16[256,256]{1,0:T(8,128)(2,1)} %param.22) | copy-start | bytes 393220
  89.7 17.1 %copy-start.3 = (bf16[256,256]{1,0:T(8,128)(2,1)S(1)}, bf16[256,256]{1,0:T(8,128)(2,1)}, u32[]{:S(2)}) copy-start(bf16[256,256]{1,0:T(8,128)(2,1)} %param.20) | copy-start | bytes 393220
  89.7 17.4 %copy-start.4 = (bf16[256,256]{1,0:T(8,128)(2,1)S(1)}, bf16[256,256]{1,0:T(8,128)(2,1)}, u32[]{:S(2)}) copy-start(bf16[256,256]{1,0:T(8,128)(2,1)} %param.21) | copy-start | bytes 393220
  91.3 14.9 %all-to-all-start = ((bf16[8,16,1,256]{3,0,2,1:T(8,128)(2,1)}), bf16[8,16,1,256]{3,0,2,1:T(8,128)(2,1)S(1)}, u32[]{:S(2)}, u32[]{:S(2)}) async-start(bf16[8,16,1,256]{3,0,2,1:T(8,128)(2,1)} %copy.50), calls=%async_computation | async-start | bytes 131072 | tf_op jit(solution)/shard_map/all_to_all | solution.py:124
  106.3 24.8 %copy-start.5 = (bf16[256,256]{1,0:T(8,128)(2,1)S(1)}, bf16[256,256]{1,0:T(8,128)(2,1)}, u32[]{:S(2)}) copy-start(bf16[256,256]{1,0:T(8,128)(2,1)} %param.24) | copy-start | bytes 393220
  106.3 24.8 %copy-start.6 = (f32[256]{0:T(256)S(1)}, f32[256]{0:T(256)}, u32[]{:S(2)}) copy-start(f32[256]{0:T(256)} %param.25) | copy-start | bytes 3076
  107.0 75.0 %copy-start.7 = (f32[128]{0:T(128)S(1)}, f32[128]{0:T(128)}, u32[]{:S(2)}) copy-start(f32[128]{0:T(128)} %param.31) | copy-start | bytes 1540
Sparse Core Ops, SparseCore 0:
  89.8 92.1 reduce-scatter.1
where the time goes:
time: 192 us; the launch traced here: 191 us
  blocking collectives  82.5 us (43%)
  waiting for transfers between devices  45.2 us (24%)
  loops' own time  15.6 us (8%)
  between operations  14.3 us (7%)
  local copies, waits for them, and re-layouts  9.78 us (5%)
  other arithmetic  8.49 us (4%)
  matrix products  8.07 us (4%)
  starting transfers between devices  7.23 us (4%)
    all_gather x1, blocking collectives, local(): right_all = lax.all_gather(right, 'dap', axis=1, tiled=True)  71.9 us
    reduce_scatter x1, waiting for transfers between devices, local(): lax.psum_scatter(jnp.einsum('sjc,sice->jie', right_all, projected, prefer...  38.2 us
    another operation x1, loops' own time, attend(): heads_out = lax.map(one_head, jnp.arange(HEADS, dtype=jnp.int32))  15.6 us
    all_to_all x1, blocking collectives, local(): lax.all_to_all(update, 'pair', split_axis=0, concat_axis=1, tiled=True)  10.6 us
    all_to_all x1, starting transfers between devices, local(): lax.all_to_all(blocks, 'pair', split_axis=1, concat_axis=0, tiled=True)  7.19 us
    all_to_all x1, waiting for transfers between devices, local(): lax.all_to_all(blocks, 'pair', split_axis=1, concat_axis=0, tiled=True)  6.99 us
    dynamic_slice x8, local copies, waits for them, and re-layouts, attend(): heads_out = lax.map(one_head, jnp.arange(HEADS, dtype=jnp.int32))  4.73 us
  transfers between devices with their start and end apart: 2, of which 2 were waited for; matrix products, arithmetic and copies ran while one was open for 7% of the time, Pallas kernels for 0%

commit v1 on v0

v1 whole, which is shorter than its diff:
```python
import jax
import jax.numpy as jnp
from jax import lax
from jax.experimental import pallas as pl
from jax.experimental.pallas import tpu as pltpu
from jax.sharding import PartitionSpec as P

GROUPS = 16
ROWS = 8
TOKENS = 128
WIDTH = 256
LANES = 128
HEADS = 8
HEAD_SIZE = 32
FACTORS = 32
C_Z = 128
F32 = jnp.float32
BF16 = jnp.bfloat16
MESH = pl.DeviceIdType.MESH


def iota(shape, axis):
    return lax.broadcasted_iota(jnp.int32, shape, axis)


def dot(a, b):
    return jnp.dot(a, b, preferred_element_type=F32)


def pack_halves(wide):
    low = wide[:, :LANES].reshape(GROUPS, ROWS, LANES)
    high = wide[:, LANES:].reshape(GROUPS, ROWS, LANES)
    return jnp.concatenate([low, high], axis=1).astype(BF16)


def unpack_halves(packed):
    tall = packed.astype(F32)
    return (
        tall[:, :ROWS].reshape(TOKENS, LANES),
        tall[:, ROWS:].reshape(TOKENS, LANES),
    )


def swap_blocks(v):
    block = iota(v[0].shape, v[0].ndim - 1) // FACTORS
    odd = block % 2 == 1
    high = block >= 2
    axis = v[0].ndim - 1
    u = [None] * 4
    for a in (0, 2):
        u[a] = jnp.where(odd, pltpu.roll(v[a + 1], 32, axis), v[a])
        u[a + 1] = jnp.where(odd, v[a + 1], pltpu.roll(v[a], 96, axis))
    w = [None] * 4
    for a in (0, 1):
        w[a] = jnp.where(high, pltpu.roll(u[a + 2], 64, axis), u[a])
        w[a + 2] = jnp.where(high, u[a + 2], pltpu.roll(u[a], 64, axis))
    return w


def kernel(
    x_hbm,
    strand_hbm,
    position_hbm,
    wq_hbm,
    wk_hbm,
    wv_hbm,
    wg_hbm,
    wo_hbm,
    bo_hbm,
    w1_hbm,
    b1_hbm,
    w2_hbm,
    b2_hbm,
    wz_hbm,
    bz_hbm,
    column_out,
    pair_out,
    x,
    strand,
    position,
    wq,
    wk,
    wv,
    wg,
    wo,
    bo,
    w1,
    b1,
    w2,
    b2,
    wz,
    bz,
    msa_send,
    msa_recv,
    upd_send,
    upd_recv,
    zbuf,
    lrbuf,
    rbuf,
    total,
    load_sem,
    msa_ssem,
    msa_rsem,
    upd_ssem,
    upd_rsem,
    z_ssem,
    z_rsem,
    lr_ssem,
    lr_rsem,
    r_ssem,
    r_rsem,
):
    d = lax.axis_index("dap")
    q = lax.axis_index("pair")
    z = lax.div(d, 2)
    xl = lax.rem(d, 2)
    other = 1 - xl

    pairs = [
        (x_hbm, x),
        (strand_hbm, strand),
        (position_hbm, position),
        (w1_hbm, w1),
        (b1_hbm, b1),
        (w2_hbm, w2),
        (b2_hbm, b2),
        (wq_hbm, wq),
        (wk_hbm, wk),
        (wv_hbm, wv),
        (wg_hbm, wg),
        (wo_hbm, wo),
        (bo_hbm, bo),
        (wz_hbm, wz),
        (bz_hbm, bz),
    ]
    loads = [pltpu.make_async_copy(a, b, load_sem.at[i]) for i, (a, b) in enumerate(pairs)]
    for load in loads:
        load.start()

    barrier = pltpu.get_barrier_semaphore()

    def greet_line(r, _):
        there = lax.rem(z + r, GROUPS)
        pl.semaphore_signal(barrier, inc=1, device_id=(there * 2 + xl, q), device_id_type=MESH)
        return 0

    def greet_plane(r, _):
        there = lax.rem(xl * GROUPS + q + r, 2 * GROUPS)
        pl.semaphore_signal(
            barrier,
            inc=1,
            device_id=(z * 2 + lax.div(there, GROUPS), lax.rem(there, GROUPS)),
            device_id_type=MESH,
        )
        return 0

    lax.fori_loop(1, GROUPS, greet_line, 0)
    lax.fori_loop(1, 2 * GROUPS, greet_plane, 0)

    loads[0].wait()
    wide = x[...].astype(F32).reshape(TOKENS, WIDTH)
    centered = wide - jnp.mean(wide, axis=-1, keepdims=True)
    spread = jnp.mean(centered * centered, axis=-1, keepdims=True)
    normed = (centered * lax.rsqrt(spread + 1e-05)).astype(BF16)

    row = iota((TOKENS, TOKENS), 0)
    col = iota((TOKENS, TOKENS), 1)
    by_residue = (col == lax.rem(row, ROWS) * GROUPS + lax.div(row, ROWS)).astype(F32).astype(BF16)
    msa_send[...] = pack_halves(dot(by_residue, normed))

    for load in loads[1:7]:
        load.wait()
    keep = strand[...].astype(F32)
    present = position[...].astype(F32)
    keep_rows = jnp.sum(
        jnp.where(col == q * ROWS + lax.div(row, GROUPS), keep, 0.0), axis=-1, keepdims=True
    )
    row4 = iota((TOKENS, 4 * LANES), 0)
    col4 = iota((TOKENS, 4 * LANES), 1)
    residue = lax.rem(row4, GROUPS)
    keep_residues = jnp.sum(
        jnp.where(col4 == d * GROUPS + residue, present, 0.0), axis=-1, keepdims=True
    )
    both = keep_rows * keep_residues
    left = ((dot(normed, w1[...]) + b1[...]) * both).astype(BF16)
    right = ((dot(normed, w2[...]) + b2[...]) * both).astype(BF16)

    factor = iota((FACTORS, 4 * LANES), 0)
    lane = iota((FACTORS, 4 * LANES), 1)
    spread_left = (lax.div(lane, GROUPS) == factor).astype(F32).astype(BF16)
    spread_right = (lax.rem(lane, FACTORS) == factor).astype(F32).astype(BF16)
    pick_row = iota((ROWS, TOKENS), 0)
    pick_col = iota((ROWS, TOKENS), 1)
    pick = (lax.div(pick_col, GROUPS) == pick_row).astype(F32).astype(BF16)
    left_lanes = jnp.where(lax.rem(col4, GROUPS) == residue, dot(left, spread_left), 0.0)
    right_lanes = jnp.where(lax.div(col4, FACTORS) == residue, dot(right, spread_right), 0.0)
    left_rows = dot(pick, left_lanes.astype(BF16))
    right_rows = dot(pick, right_lanes.astype(BF16))

    def fold(rows):
        tiles = [rows[:, LANES * g : LANES * (g + 1)] for g in range(4)]
        return jnp.concatenate(tiles, axis=0).reshape(2, 2 * ROWS, LANES).astype(BF16)

    zbuf[:, 0:2] = jnp.broadcast_to(fold(left_rows)[None], (GROUPS, 2, 2 * ROWS, LANES))
    zbuf[pl.ds(z, 1), 2:4] = fold(right_rows)[None]

    pl.semaphore_wait(barrier, GROUPS - 1 + 2 * GROUPS - 1)

    def send_msa(r, _):
        there = lax.rem(q + r, GROUPS)
        pltpu.make_async_remote_copy(
            src_ref=msa_send.at[there],
            dst_ref=msa_recv.at[q],
            send_sem=msa_ssem,
            recv_sem=msa_rsem,
            device_id=(d, there),
            device_id_type=MESH,
        ).start()
        return 0

    lax.fori_loop(1, GROUPS, send_msa, 0)
    pltpu.make_async_copy(msa_send.at[q], msa_recv.at[q], msa_rsem).start()

    def send_line(r, _):
        there = lax.rem(z + r, GROUPS)
        pltpu.make_async_remote_copy(
            src_ref=zbuf.at[z, pl.ds(2, 2)],
            dst_ref=zbuf.at[z, pl.ds(2, 2)],
            send_sem=z_ssem,
            recv_sem=z_rsem.at[z],
            device_id=(there * 2 + xl, q),
            device_id_type=MESH,
        ).start()
        return 0

    lax.fori_loop(1, GROUPS, send_line, 0)

    def pass_on(r, _):
        there = lax.rem(z + r, GROUPS)

        @pl.when(r > 0)
        def _():
            pltpu.make_async_copy(
                zbuf.at[there, pl.ds(2, 2)], zbuf.at[there, pl.ds(2, 2)], z_rsem.at[there]
            ).wait()

        @pl.when(there != q)
        def _():
            pltpu.make_async_remote_copy(
                src_ref=zbuf.at[there],
                dst_ref=lrbuf.at[q],
                send_sem=lr_ssem,
                recv_sem=lr_rsem,
                device_id=(d, there),
                device_id_type=MESH,
            ).start()

        @pl.when(there == q)
        def _():
            pltpu.make_async_copy(zbuf.at[there], lrbuf.at[q], lr_rsem).start()

        pltpu.make_async_remote_copy(
            src_ref=zbuf.at[there, pl.ds(2, 2)],
            dst_ref=rbuf.at[q],
            send_sem=r_ssem,
            recv_sem=r_rsem,
            device_id=(z * 2 + other, there),
            device_id_type=MESH,
        ).start()
        return 0

    lax.fori_loop(0, 1, pass_on, 0)

    for load in loads[7:11]:
        load.wait()
    pltpu.make_async_copy(msa_recv, msa_recv, msa_rsem).wait()
    items = jnp.concatenate(unpack_halves(msa_recv[...]), axis=1).astype(BF16)
    queries = (dot(items, wq[...]) * HEAD_SIZE ** (-0.5)).astype(BF16)
    keys = dot(items, wk[...]).astype(BF16)
    values = dot(items, wv[...]).astype(BF16)
    gates = jax.nn.sigmoid(dot(items, wg[...]))
    head = lax.div(iota((TOKENS, WIDTH), 1), HEAD_SIZE)
    zero = jnp.zeros((TOKENS, WIDTH), BF16)
    one = jnp.ones((TOKENS, WIDTH), BF16)
    queries_by_head = jnp.concatenate(
        [jnp.where(head == h, queries, zero) for h in range(HEADS)], axis=0
    )
    values_by_head = jnp.concatenate(
        [jnp.where(head == h, values, zero) for h in range(HEADS)], axis=0
    )
    ones_by_head = jnp.concatenate([jnp.where(head == h, one, zero) for h in range(HEADS)], axis=0)
    scores = lax.dot_general(
        queries_by_head, keys, (((1,), (1,)), ((), ())), preferred_element_type=F32
    ) + (keep - 1.0) * 1e9
    weights = jnp.exp(scores - jnp.max(scores, axis=-1, keepdims=True)).astype(BF16)
    weights = jnp.concatenate(
        [weights[h * TOKENS : (h + 1) * TOKENS] for h in range(HEADS)], axis=1
    )
    mixed = dot(weights, values_by_head) / dot(weights, ones_by_head)
    attended = (mixed * gates).astype(BF16)
    loads[11].wait()
    loads[12].wait()
    upd_send[...] = pack_halves(dot(attended, wo[...]) + bo[...])

    def send_update(r, _):
        there = lax.rem(q + r, GROUPS)
        pltpu.make_async_remote_copy(
            src_ref=upd_send.at[there],
            dst_ref=upd_recv.at[q],
            send_sem=upd_ssem,
            recv_sem=upd_rsem,
            device_id=(d, there),
            device_id_type=MESH,
        ).start()
        return 0

    lax.fori_loop(1, GROUPS, send_update, 0)
    pltpu.make_async_copy(upd_send.at[q], upd_recv.at[q], upd_rsem).start()

    lax.fori_loop(1, GROUPS, pass_on, 0)

    pltpu.make_async_copy(upd_recv, upd_recv, upd_rsem).wait()
    by_row = (col == lax.rem(row, GROUPS) * ROWS + lax.div(row, GROUPS)).astype(F32).astype(BF16)
    update = jnp.concatenate(unpack_halves(upd_recv[...]), axis=1).astype(BF16)
    column_out[...] = dot(by_row, update).astype(BF16).reshape(ROWS, GROUPS, WIDTH)

    loads[13].wait()
    loads[14].wait()
    kept = jnp.sum(keep)
    pltpu.make_async_copy(lrbuf, lrbuf, lr_rsem).wait()
    left_t = jnp.concatenate(
        [tile.T for a in range(2) for tile in unpack_halves(lrbuf[:, a])], axis=0
    ).astype(BF16)

    def finish(half, pieces, place):
        rights = jnp.concatenate(
            [tile for piece in pieces for tile in unpack_halves(piece)], axis=1
        ).astype(BF16)
        outer = dot(left_t, rights).reshape(FACTORS, GROUPS, 4 * LANES)
        rows = [[None] * 8 for _ in range(GROUPS)]
        for c in range(8):
            for j in range(4):
                moved = swap_blocks(
                    [outer[4 * c + a, :, LANES * j : LANES * (j + 1)] for a in range(4)]
                )
                for b in range(4):
                    rows[4 * j + b][c] = moved[b].astype(BF16)
        flat = jnp.concatenate([jnp.concatenate(r, axis=1) for r in rows], axis=0)
        sums = dot(flat, wz[...])
        for k in range(GROUPS):
            total[half, pl.ds(k, GROUPS, stride=GROUPS), :] = sums[GROUPS * k : GROUPS * (k + 1)]
        pair_out[:, pl.ds(pl.multiple_of(place * GROUPS, GROUPS), GROUPS), :] = (
            (total[half] / kept + bz[...]).astype(BF16).reshape(GROUPS, GROUPS, C_Z)
        )

    finish(0, [lrbuf[:, 2], lrbuf[:, 3]], xl)
    pltpu.make_async_copy(rbuf, rbuf, r_rsem).wait()
    finish(1, [rbuf[:, 0], rbuf[:, 1]], other)

    some = pl.ds(0, GROUPS - 1)

    def sent(ref, sem):
        pltpu.make_async_copy(ref, ref, sem).wait()

    sent(msa_send.at[some], msa_ssem)
    sent(upd_send.at[some], upd_ssem)
    sent(zbuf.at[some, pl.ds(2, 2)], z_ssem)
    sent(zbuf.at[some], lr_ssem)
    sent(rbuf, r_ssem)


def local(
    alignment_activity,
    existing_strand_flags,
    existing_position_flags,
    asking_vector_map,
    lookup_address_map,
    content_vector_map,
    sigmoid_switch_map,
    final_mixing_map,
    final_offset_vector,
    first_factor_map,
    first_factor_offset,
    second_factor_map,
    second_factor_offset,
    couple_mixing_map,
    couple_change_offset,
):
    args = (
        alignment_activity,
        existing_strand_flags.reshape(1, -1),
        existing_position_flags.reshape(1, -1),
        asking_vector_map,
        lookup_address_map,
        content_vector_map,
        sigmoid_switch_map,
        final_mixing_map,
        final_offset_vector.reshape(1, -1),
        first_factor_map,
        first_factor_offset.reshape(1, -1),
        second_factor_map,
        second_factor_offset.reshape(1, -1),
        couple_mixing_map,
        couple_change_offset.reshape(1, -1),
    )
    piece = (2 * ROWS, LANES)
    return pl.pallas_call(
        kernel,
        out_shape=(
            jax.ShapeDtypeStruct((ROWS, GROUPS, WIDTH), BF16),
            jax.ShapeDtypeStruct((GROUPS, 2 * GROUPS, C_Z), BF16),
        ),
        in_specs=[pl.BlockSpec(memory_space=pl.ANY)] * len(args),
        out_specs=[pl.BlockSpec(memory_space=pltpu.VMEM)] * 2,
        scratch_shapes=[pltpu.VMEM(a.shape, a.dtype) for a in args]
        + [
            pltpu.VMEM((GROUPS, *piece), BF16),
            pltpu.VMEM((GROUPS, *piece), BF16),
            pltpu.VMEM((GROUPS, *piece), BF16),
            pltpu.VMEM((GROUPS, *piece), BF16),
            pltpu.VMEM((GROUPS, 4, *piece), BF16),
            pltpu.VMEM((GROUPS, 4, *piece), BF16),
            pltpu.VMEM((GROUPS, 2, *piece), BF16),
            pltpu.VMEM((2, WIDTH, C_Z), F32),
            pltpu.SemaphoreType.DMA((len(args),)),
            pltpu.SemaphoreType.DMA,
            pltpu.SemaphoreType.DMA,
            pltpu.SemaphoreType.DMA,
            pltpu.SemaphoreType.DMA,
            pltpu.SemaphoreType.DMA,
            pltpu.SemaphoreType.DMA((GROUPS,)),
            pltpu.SemaphoreType.DMA,
            pltpu.SemaphoreType.DMA,
            pltpu.SemaphoreType.DMA,
            pltpu.SemaphoreType.DMA,
        ],
        compiler_params=pltpu.CompilerParams(
            collective_id=0, has_side_effects=True, vmem_limit_bytes=32 * 1024 * 1024
        ),
        name="column_attention_and_outer_mean",
    )(*args)


def solution(mesh):
    return jax.shard_map(
        local,
        mesh=mesh,
        in_specs=(P("pair", "dap", None),) + (P(),) * 14,
        out_specs=(P("pair", "dap", None), P("dap", "pair", None)),
        check_vma=False,
    )
```

time: 192 us -> 43.7 us (0.23)
  the two profiles are of different devices: /device:TPU:32 before, /device:TPU:25 now
where the time goes in v1:
time: 43.7 us; the launch traced here: 43.4 us
  Pallas kernels  34.2 us (78%)
  local copies, waits for them, and re-layouts  8.46 us (19%)
  between operations  0.76 us (2%)
    pallas_call x1, Pallas kernels, local(): pl.pallas_call(kernel, out_shape=(jax.ShapeDtypeStruct((ROWS, GROUPS, WID...  34.2 us
    unnamed x30, local copies, waits for them, and re-layouts  8.46 us

profile of v1, /device:TPU:25, one launch (start us, length us, event | category | flops | bytes accessed | tf_op | source)
XLA Modules:
  0.0 43.4 jit_solution(4795819319112491232)
XLA Ops:
  0.6 0.0 copy-start.1
  0.6 0.9 %copy.17.w1_hbm = bf16[256,32]{1,0:T(8,128)(2,1)S(1)} copy(bf16[256,32]{0,1:T(8,128)(2,1)} %param.24) | data formatting | bytes 32768 | tf_op args[9]
  1.5 0.0 copy-start.7
  1.5 0.0 copy-start.8
  1.5 0.0 copy-start.9
  1.5 0.0 copy-start.10
  1.6 0.0 copy-start.11
  1.6 0.0 copy-start.12
  1.6 0.9 %copy.18.w2_hbm = bf16[256,32]{1,0:T(8,128)(2,1)S(1)} copy(bf16[256,32]{0,1:T(8,128)(2,1)} %param.26) | data formatting | bytes 32768 | tf_op args[11]
  2.4 0.0 copy-done.1
  2.5 0.0 copy-done.7
  2.5 0.0 copy-done.8
  2.5 0.0 copy-done.9
  2.5 0.0 copy-done.10
  2.5 0.0 copy-done.11
  2.5 0.0 copy-done.12
  2.5 0.0 copy-start
  2.5 0.9 %copy-done = bf16[1024,128]{1,0:T(8,128)(2,1)S(1)} copy-done((bf16[1024,128]{1,0:T(8,128)(2,1)S(1)}, bf16[1024,128]{1,0:T(8,128)(2,1)}, u32[]{:S(2)}) %copy-start) | copy-done | bytes 262168
  3.5 0.0 copy-start.2
  3.5 0.9 %copy-done.2 = bf16[256,256]{1,0:T(8,128)(2,1)S(1)} copy-done((bf16[256,256]{1,0:T(8,128)(2,1)S(1)}, bf16[256,256]{1,0:T(8,128)(2,1)}, u32[]{:S(2)}) %copy-start.2) | copy-done | bytes 131096
  4.4 0.0 copy-start.3
  4.4 0.9 %copy-done.3 = bf16[256,256]{1,0:T(8,128)(2,1)S(1)} copy-done((bf16[256,256]{1,0:T(8,128)(2,1)S(1)}, bf16[256,256]{1,0:T(8,128)(2,1)}, u32[]{:S(2)}) %copy-start.3) | copy-done | bytes 131096
  5.3 0.0 copy-start.4
  5.3 0.9 %copy-done.4 = bf16[256,256]{1,0:T(8,128)(2,1)S(1)} copy-done((bf16[256,256]{1,0:T(8,128)(2,1)S(1)}, bf16[256,256]{1,0:T(8,128)(2,1)}, u32[]{:S(2)}) %copy-start.4) | copy-done | bytes 131096
  6.2 0.0 copy-start.5
  6.2 0.9 %copy-done.5 = bf16[256,256]{1,0:T(8,128)(2,1)S(1)} copy-done((bf16[256,256]{1,0:T(8,128)(2,1)S(1)}, bf16[256,256]{1,0:T(8,128)(2,1)}, u32[]{:S(2)}) %copy-start.5) | copy-done | bytes 131096
  7.1 0.0 copy-start.6
  7.1 0.8 %copy-done.6 = bf16[8,16,256]{2,1,0:T(8,128)(2,1)S(1)} copy-done((bf16[8,16,256]{2,1,0:T(8,128)(2,1)S(1)}, bf16[8,16,256]{2,1,0:T(8,128)(2,1)}, u32[]{:S(2)}) %copy-start.6) | copy-done | bytes 65560
  7.9 34.2 %column_attention_and_outer_mean.1 = (bf16[8,16,256]{2,1,0:T(8,128)(2,1)S(1)}, bf16[16,32,128]{2,1,0:T(8,128)(2,1)S(1)}) custom-call(bf16[8,16,256]{2,1,0:T(8,128)(2,1)S(1)} %copy-done.6, s32[1,128]{1,0:T(1,128)S(1)} %bitcast.8, s32[1,512]{1,0:T(1,128)S(1)} %bitcast.6, bf16[256,256]{1,0:T(8,128)(2,1)S(1)} %copy-done.1, bf16[256,256]{1,0:T(8,128)(2,1)S(1)} %copy-done.2, ...), custom_call_target="tpu_custom_call" | custom-call | tf_op jit(solution)/shard_map/column_attention_and_outer_mean/pallas_call | solution.py:407
  42.1 0.6 %copy.21 = bf16[8,16,256]{2,1,0:T(8,128)(2,1)} copy(bf16[8,16,256]{2,1,0:T(8,128)(2,1)S(1)} %get-tuple-element.4) | data formatting | bytes 131072
  42.7 0.7 %copy.22 = bf16[16,32,128]{2,1,0:T(8,128)(2,1)} copy(bf16[16,32,128]{2,1,0:T(8,128)(2,1)S(1)} %get-tuple-element.5) | data formatting | bytes 262144
Async XLA Ops:
  0.6 1.8 %copy-start.1 = (bf16[256,256]{1,0:T(8,128)(2,1)S(1)}, bf16[256,256]{1,0:T(8,128)(2,1)}, u32[]{:S(2)}) copy-start(bf16[256,256]{1,0:T(8,128)(2,1)} %wq_hbm.1) | copy-start | bytes 393220
  1.5 0.9 %copy-start.7 = (s32[512]{0:T(512)S(1)}, s32[512]{0:T(512)}, u32[]{:S(2)}) copy-start(s32[512]{0:T(512)} %param.17) | copy-start | bytes 6148
  1.5 0.9 %copy-start.8 = (f32[256]{0:T(256)S(1)}, f32[256]{0:T(256)}, u32[]{:S(2)}) copy-start(f32[256]{0:T(256)} %param.23) | copy-start | bytes 3076
  1.5 0.9 %copy-start.9 = (s32[128]{0:T(128)S(1)}, s32[128]{0:T(128)}, u32[]{:S(2)}) copy-start(s32[128]{0:T(128)} %param.16) | copy-start | bytes 1540
  1.5 0.9 %copy-start.10 = (f32[32]{0:T(128)S(1)}, f32[32]{0:T(128)}, u32[]{:S(2)}) copy-start(f32[32]{0:T(128)} %param.25) | copy-start | bytes 388
  1.6 0.9 %copy-start.11 = (f32[32]{0:T(128)S(1)}, f32[32]{0:T(128)}, u32[]{:S(2)}) copy-start(f32[32]{0:T(128)} %param.27) | copy-start | bytes 388
  1.6 0.9 %copy-start.12 = (f32[128]{0:T(128)S(1)}, f32[128]{0:T(128)}, u32[]{:S(2)}) copy-start(f32[128]{0:T(128)} %param.29) | copy-start | bytes 1540
  2.5 1.0 %copy-start = (bf16[1024,128]{1,0:T(8,128)(2,1)S(1)}, bf16[1024,128]{1,0:T(8,128)(2,1)}, u32[]{:S(2)}) copy-start(bf16[1024,128]{1,0:T(8,128)(2,1)} %wz_hbm.1) | copy-start | bytes 786436
  3.5 0.9 %copy-start.2 = (bf16[256,256]{1,0:T(8,128)(2,1)S(1)}, bf16[256,256]{1,0:T(8,128)(2,1)}, u32[]{:S(2)}) copy-start(bf16[256,256]{1,0:T(8,128)(2,1)} %wk_hbm.1) | copy-start | bytes 393220
  4.4 0.9 %copy-start.3 = (bf16[256,256]{1,0:T(8,128)(2,1)S(1)}, bf16[256,256]{1,0:T(8,128)(2,1)}, u32[]{:S(2)}) copy-start(bf16[256,256]{1,0:T(8,128)(2,1)} %wv_hbm.1) | copy-start | bytes 393220
  5.3 0.9 %copy-start.4 = (bf16[256,256]{1,0:T(8,128)(2,1)S(1)}, bf16[256,256]{1,0:T(8,128)(2,1)}, u32[]{:S(2)}) copy-start(bf16[256,256]{1,0:T(8,128)(2,1)} %wg_hbm.1) | copy-start | bytes 393220
  6.2 0.9 %copy-start.5 = (bf16[256,256]{1,0:T(8,128)(2,1)S(1)}, bf16[256,256]{1,0:T(8,128)(2,1)}, u32[]{:S(2)}) copy-start(bf16[256,256]{1,0:T(8,128)(2,1)} %wo_hbm.1) | copy-start | bytes 393220
  7.1 0.8 %copy-start.6 = (bf16[8,16,256]{2,1,0:T(8,128)(2,1)S(1)}, bf16[8,16,256]{2,1,0:T(8,128)(2,1)}, u32[]{:S(2)}) copy-start(bf16[8,16,256]{2,1,0:T(8,128)(2,1)} %x_hbm.1) | copy-start | bytes 196612

commit v2 on v1

--- a/solution.py
+++ b/solution.py
@@ -14,6 +14,7 @@
 HEAD_SIZE = 32
 FACTORS = 32
 C_Z = 128
+EARLY = 8
 F32 = jnp.float32
 BF16 = jnp.bfloat16
 MESH = pl.DeviceIdType.MESH
@@ -25,6 +26,10 @@
 
 def dot(a, b):
     return jnp.dot(a, b, preferred_element_type=F32)
+
+
+def dot_t(a, b):
+    return lax.dot_general(a, b, (((1,), (1,)), ((), ())), preferred_element_type=F32)
 
 
 def pack_halves(wide):
@@ -95,7 +100,6 @@
     upd_send,
     upd_recv,
     zbuf,
-    lrbuf,
     rbuf,
     total,
     load_sem,
@@ -105,10 +109,9 @@
     upd_rsem,
     z_ssem,
     z_rsem,
-    lr_ssem,
-    lr_rsem,
     r_ssem,
     r_rsem,
+    ready,
 ):
     d = lax.axis_index("dap")
     q = lax.axis_index("pair")
@@ -139,9 +142,11 @@
 
     barrier = pltpu.get_barrier_semaphore()
 
-    def greet_line(r, _):
-        there = lax.rem(z + r, GROUPS)
-        pl.semaphore_signal(barrier, inc=1, device_id=(there * 2 + xl, q), device_id_type=MESH)
+    def line(there):
+        return (there * 2 + xl, q)
+
+    def greet_line(there, _):
+        pl.semaphore_signal(barrier, inc=1, device_id=line(there), device_id_type=MESH)
         return 0
 
     def greet_plane(r, _):
@@ -154,8 +159,8 @@
         )
         return 0
 
-    lax.fori_loop(1, GROUPS, greet_line, 0)
     lax.fori_loop(1, 2 * GROUPS, greet_plane, 0)
+    lax.fori_loop(z + 1, GROUPS, greet_line, 0)
 
     loads[0].wait()
     wide = x[...].astype(F32).reshape(TOKENS, WIDTH)
@@ -166,8 +171,6 @@
     row = iota((TOKENS, TOKENS), 0)
     col = iota((TOKENS, TOKENS), 1)
     by_residue = (col == lax.rem(row, ROWS) * GROUPS + lax.div(row, ROWS)).astype(F32).astype(BF16)
-    msa_send[...] = pack_halves(dot(by_residue, normed))
-
     for load in loads[1:7]:
         load.wait()
     keep = strand[...].astype(F32)
@@ -182,8 +185,8 @@
         jnp.where(col4 == d * GROUPS + residue, present, 0.0), axis=-1, keepdims=True
     )
     both = keep_rows * keep_residues
-    left = ((dot(normed, w1[...]) + b1[...]) * both).astype(BF16)
-    right = ((dot(normed, w2[...]) + b2[...]) * both).astype(BF16)
+    left = ((dot_t(normed, w1[...]) + b1[...]) * both).astype(BF16)
+    right = ((dot_t(normed, w2[...]) + b2[...]) * both).astype(BF16)
 
     factor = iota((FACTORS, 4 * LANES), 0)
     lane = iota((FACTORS, 4 * LANES), 1)
@@ -194,17 +197,40 @@
     pick = (lax.div(pick_col, GROUPS) == pick_row).astype(F32).astype(BF16)
     left_lanes = jnp.where(lax.rem(col4, GROUPS) == residue, dot(left, spread_left), 0.0)
     right_lanes = jnp.where(lax.div(col4, FACTORS) == residue, dot(right, spread_right), 0.0)
-    left_rows = dot(pick, left_lanes.astype(BF16))
     right_rows = dot(pick, right_lanes.astype(BF16))
 
     def fold(rows):
         tiles = [rows[:, LANES * g : LANES * (g + 1)] for g in range(4)]
-        return jnp.concatenate(tiles, axis=0).reshape(2, 2 * ROWS, LANES).astype(BF16)
-
-    zbuf[:, 0:2] = jnp.broadcast_to(fold(left_rows)[None], (GROUPS, 2, 2 * ROWS, LANES))
-    zbuf[pl.ds(z, 1), 2:4] = fold(right_rows)[None]
-
-    pl.semaphore_wait(barrier, GROUPS - 1 + 2 * GROUPS - 1)
+        return jnp.concatenate(tiles, axis=0).reshape(1, 2, 2 * ROWS, LANES).astype(BF16)
+
+    zbuf[pl.ds(z, 1)] = fold(right_rows)
+    msa_send[:, 0] = pack_halves(dot(by_residue, normed))
+    left_rows = dot(pick, left_lanes.astype(BF16))
+    msa_send[:, 1:3] = jnp.broadcast_to(fold(left_rows), (GROUPS, 2, 2 * ROWS, LANES))
+
+    pl.semaphore_wait(barrier, 2 * GROUPS - 1 + z)
+
+    def send_line(there, _):
+        pltpu.make_async_remote_copy(
+            src_ref=zbuf.at[z],
+            dst_ref=zbuf.at[z],
+            send_sem=z_ssem,
+            recv_sem=z_rsem.at[z],
+            device_id=line(there),
+            device_id_type=MESH,
+        ).start()
+        return 0
+
+    def answer_line(there, _):
+        pl.semaphore_signal(ready.at[z], inc=1, device_id=line(there), device_id_type=MESH)
+        return 0
+
+    def send_when_ready(there, _):
+        pl.semaphore_wait(ready.at[there], 1)
+        return send_line(there, 0)
+
+    lax.fori_loop(0, z, send_line, 0)
+    lax.fori_loop(0, z, answer_line, 0)
 
     def send_msa(r, _):
         there = lax.rem(q + r, GROUPS)
@@ -221,60 +247,53 @@
     lax.fori_loop(1, GROUPS, send_msa, 0)
     pltpu.make_async_copy(msa_send.at[q], msa_recv.at[q], msa_rsem).start()
 
-    def send_line(r, _):
-        there = lax.rem(z + r, GROUPS)
-        pltpu.make_async_remote_copy(
-            src_ref=zbuf.at[z, pl.ds(2, 2)],
-            dst_ref=zbuf.at[z, pl.ds(2, 2)],
-            send_sem=z_ssem,
-            recv_sem=z_rsem.at[z],
-            device_id=(there * 2 + xl, q),
-            device_id_type=MESH,
-        ).start()
-        return 0
-
-    lax.fori_loop(1, GROUPS, send_line, 0)
-
-    def pass_on(r, _):
-        there = lax.rem(z + r, GROUPS)
-
-        @pl.when(r > 0)
-        def _():
-            pltpu.make_async_copy(
-                zbuf.at[there, pl.ds(2, 2)], zbuf.at[there, pl.ds(2, 2)], z_rsem.at[there]
-            ).wait()
-
+    def pass_on(there):
         @pl.when(there != q)
         def _():
             pltpu.make_async_remote_copy(
                 src_ref=zbuf.at[there],
-                dst_ref=lrbuf.at[q],
-                send_sem=lr_ssem,
-                recv_sem=lr_rsem,
+                dst_ref=rbuf.at[xl, q],
+                send_sem=r_ssem,
+                recv_sem=r_rsem.at[xl],
                 device_id=(d, there),
                 device_id_type=MESH,
             ).start()
 
         @pl.when(there == q)
         def _():
-            pltpu.make_async_copy(zbuf.at[there], lrbuf.at[q], lr_rsem).start()
+            pltpu.make_async_copy(zbuf.at[there], rbuf.at[xl, q], r_rsem.at[xl]).start()
 
         pltpu.make_async_remote_copy(
-            src_ref=zbuf.at[there, pl.ds(2, 2)],
-            dst_ref=rbuf.at[q],
+            src_ref=zbuf.at[there],
+            dst_ref=rbuf.at[xl, q],
             send_sem=r_ssem,
-            recv_sem=r_rsem,
+            recv_sem=r_rsem.at[xl],
             device_id=(z * 2 + other, there),
             device_id_type=MESH,
         ).start()
-        return 0
-
-    lax.fori_loop(0, 1, pass_on, 0)
+
+    pass_on(z)
+
+    early = z < EARLY
+
+    def exchange(i, _):
+        there = jnp.where(early, jnp.where(i < EARLY, i, 23 - i), lax.rem(i + EARLY, GROUPS))
+
+        @pl.when(jnp.logical_and(early, there >= EARLY))
+        def _():
+            send_when_ready(there, 0)
+
+        @pl.when(there != z)
+        def _():
+            pltpu.make_async_copy(zbuf.at[there], zbuf.at[there], z_rsem.at[there]).wait()
+            pass_on(there)
+
+        return 0
 
     for load in loads[7:11]:
         load.wait()
     pltpu.make_async_copy(msa_recv, msa_recv, msa_rsem).wait()
-    items = jnp.concatenate(unpack_halves(msa_recv[...]), axis=1).astype(BF16)
+    items = jnp.concatenate(unpack_halves(msa_recv[:, 0]), axis=1).astype(BF16)
     queries = (dot(items, wq[...]) * HEAD_SIZE ** (-0.5)).astype(BF16)
     keys = dot(items, wk[...]).astype(BF16)
     values = dot(items, wv[...]).astype(BF16)
@@ -289,9 +308,7 @@
         [jnp.where(head == h, values, zero) for h in range(HEADS)], axis=0
     )
     ones_by_head = jnp.concatenate([jnp.where(head == h, one, zero) for h in range(HEADS)], axis=0)
-    scores = lax.dot_general(
-        queries_by_head, keys, (((1,), (1,)), ((), ())), preferred_element_type=F32
-    ) + (keep - 1.0) * 1e9
+    scores = dot_t(queries_by_head, keys) + (keep - 1.0) * 1e9
     weights = jnp.exp(scores - jnp.max(scores, axis=-1, keepdims=True)).astype(BF16)
     weights = jnp.concatenate(
         [weights[h * TOKENS : (h + 1) * TOKENS] for h in range(HEADS)], axis=1
@@ -317,24 +334,27 @@
     lax.fori_loop(1, GROUPS, send_update, 0)
     pltpu.make_async_copy(upd_send.at[q], upd_recv.at[q], upd_rsem).start()
 
-    lax.fori_loop(1, GROUPS, pass_on, 0)
+    lax.fori_loop(z + 1, jnp.where(early, EARLY, GROUPS), send_when_ready, 0)
+    lax.fori_loop(0, EARLY, exchange, 0)
 
     pltpu.make_async_copy(upd_recv, upd_recv, upd_rsem).wait()
     by_row = (col == lax.rem(row, GROUPS) * ROWS + lax.div(row, GROUPS)).astype(F32).astype(BF16)
     update = jnp.concatenate(unpack_halves(upd_recv[...]), axis=1).astype(BF16)
     column_out[...] = dot(by_row, update).astype(BF16).reshape(ROWS, GROUPS, WIDTH)
 
+    left_t = jnp.concatenate(
+        [tile.T for a in (1, 2) for tile in unpack_halves(msa_recv[:, a])], axis=0
+    ).astype(BF16)
     loads[13].wait()
     loads[14].wait()
     kept = jnp.sum(keep)
-    pltpu.make_async_copy(lrbuf, lrbuf, lr_rsem).wait()
-    left_t = jnp.concatenate(
-        [tile.T for a in range(2) for tile in unpack_halves(lrbuf[:, a])], axis=0
-    ).astype(BF16)
-
-    def finish(half, pieces, place):
+
+    lax.fori_loop(EARLY, GROUPS, exchange, 0)
+
+    for half in range(2):
+        pltpu.make_async_copy(rbuf.at[half], rbuf.at[half], r_rsem.at[half]).wait()
         rights = jnp.concatenate(
-            [tile for piece in pieces for tile in unpack_halves(piece)], axis=1
+            [tile for a in range(2) for tile in unpack_halves(rbuf[half, :, a])], axis=1
         ).astype(BF16)
         outer = dot(left_t, rights).reshape(FACTORS, GROUPS, 4 * LANES)
         rows = [[None] * 8 for _ in range(GROUPS)]
@@ -349,14 +369,10 @@
         sums = dot(flat, wz[...])
         for k in range(GROUPS):
             total[half, pl.ds(k, GROUPS, stride=GROUPS), :] = sums[GROUPS * k : GROUPS * (k + 1)]
-        pair_out[:, pl.ds(pl.multiple_of(place * GROUPS, GROUPS), GROUPS), :] = (
+        pair_out[:, half * GROUPS : (half + 1) * GROUPS, :] = (
             (total[half] / kept + bz[...]).astype(BF16).reshape(GROUPS, GROUPS, C_Z)
         )
 
-    finish(0, [lrbuf[:, 2], lrbuf[:, 3]], xl)
-    pltpu.make_async_copy(rbuf, rbuf, r_rsem).wait()
-    finish(1, [rbuf[:, 0], rbuf[:, 1]], other)
-
     some = pl.ds(0, GROUPS - 1)
 
     def sent(ref, sem):
@@ -364,9 +380,9 @@
 
     sent(msa_send.at[some], msa_ssem)
     sent(upd_send.at[some], upd_ssem)
-    sent(zbuf.at[some, pl.ds(2, 2)], z_ssem)
-    sent(zbuf.at[some], lr_ssem)
-    sent(rbuf, r_ssem)
+    sent(zbuf.at[some], z_ssem)
+    sent(zbuf, r_ssem)
+    sent(zbuf.at[some], r_ssem)
 
 
 def local(
@@ -396,9 +412,9 @@
         sigmoid_switch_map,
         final_mixing_map,
         final_offset_vector.reshape(1, -1),
-        first_factor_map,
+        first_factor_map.T,
         first_factor_offset.reshape(1, -1),
-        second_factor_map,
+        second_factor_map.T,
         second_factor_offset.reshape(1, -1),
         couple_mixing_map,
         couple_change_offset.reshape(1, -1),
@@ -414,13 +430,12 @@
         out_specs=[pl.BlockSpec(memory_space=pltpu.VMEM)] * 2,
         scratch_shapes=[pltpu.VMEM(a.shape, a.dtype) for a in args]
         + [
+            pltpu.VMEM((GROUPS, 3, *piece), BF16),
+            pltpu.VMEM((GROUPS, 3, *piece), BF16),
             pltpu.VMEM((GROUPS, *piece), BF16),
             pltpu.VMEM((GROUPS, *piece), BF16),
-            pltpu.VMEM((GROUPS, *piece), BF16),
-            pltpu.VMEM((GROUPS, *piece), BF16),
-            pltpu.VMEM((GROUPS, 4, *piece), BF16),
-            pltpu.VMEM((GROUPS, 4, *piece), BF16),
             pltpu.VMEM((GROUPS, 2, *piece), BF16),
+            pltpu.VMEM((2, GROUPS, 2, *piece), BF16),
             pltpu.VMEM((2, WIDTH, C_Z), F32),
             pltpu.SemaphoreType.DMA((len(args),)),
             pltpu.SemaphoreType.DMA,
@@ -430,12 +445,11 @@
             pltpu.SemaphoreType.DMA,
             pltpu.SemaphoreType.DMA((GROUPS,)),
             pltpu.SemaphoreType.DMA,
-            pltpu.SemaphoreType.DMA,
-            pltpu.SemaphoreType.DMA,
-            pltpu.SemaphoreType.DMA,
+            pltpu.SemaphoreType.DMA((2,)),
+            pltpu.SemaphoreType.REGULAR((GROUPS,)),
         ],
         compiler_params=pltpu.CompilerParams(
-            collective_id=0, has_side_effects=True, vmem_limit_bytes=32 * 1024 * 1024
+            collective_id=0, has_side_effects=True, vmem_limit_bytes=60 * 1024 * 1024
         ),
         name="column_attention_and_outer_mean",
     )(*args)

time: 43.7 us -> 36.4 us (0.83)
  the two profiles are of different devices: /device:TPU:25 before, /device:TPU:393 now
where the time goes in v2:
time: 36.4 us; the launch traced here: 36.2 us
  Pallas kernels  33.4 us (92%)
  local copies, waits for them, and re-layouts  2.17 us (6%)
  between operations  0.65 us (2%)
    pallas_call x1, Pallas kernels, local(): pl.pallas_call(kernel, out_shape=(jax.ShapeDtypeStruct((ROWS, GROUPS, WID...  33.4 us
    unnamed x4, local copies, waits for them, and re-layouts  2.17 us

profile of v2, /device:TPU:393, one launch (start us, length us, event | category | flops | bytes accessed | tf_op | source)
XLA Modules:
  0.0 36.2 jit_solution(2563843972282507190)
XLA Ops:
  0.6 33.4 %column_attention_and_outer_mean.1 = (bf16[8,16,256]{2,1,0:T(8,128)(2,1)}, bf16[16,32,128]{2,1,0:T(8,128)(2,1)}) custom-call(bf16[8,16,256]{2,1,0:T(8,128)(2,1)} %x_hbm.1, s32[1,128]{1,0:T(1,128)} %bitcast.12, s32[1,512]{1,0:T(1,128)} %bitcast.10, bf16[256,256]{1,0:T(8,128)(2,1)} %wq_hbm.1, bf16[256,256]{1,0:T(8,128)(2,1)} %wk_hbm.1, ...), custom_call_target="tpu_custom_call" | custom-call | tf_op jit(solution)/shard_map/column_attention_and_outer_mean/pallas_call | solution.py:423
  34.0 0.0 copy-start
  34.1 1.5 %copy.19 = bf16[8,16,256]{2,1,0:T(8,128)(2,1)} copy(bf16[8,16,256]{2,1,0:T(8,128)(2,1)} %get-tuple-element.4) | data formatting | bytes 131072
  35.6 0.0 copy-done
  35.6 0.7 %copy.20 = bf16[16,32,128]{2,1,0:T(8,128)(2,1)} copy(bf16[16,32,128]{2,1,0:T(8,128)(2,1)S(1)} %copy-done) | data formatting | bytes 262144
Async XLA Ops:
  34.0 1.5 %copy-start = (bf16[16,32,128]{2,1,0:T(8,128)(2,1)S(1)}, bf16[16,32,128]{2,1,0:T(8,128)(2,1)}, u32[]{:S(2)}) copy-start(bf16[16,32,128]{2,1,0:T(8,128)(2,1)} %get-tuple-element.5) | copy-start | bytes 393220

commit v3 on v2

--- a/solution.py
+++ b/solution.py
@@ -15,6 +15,7 @@
 FACTORS = 32
 C_Z = 128
 EARLY = 8
+NEAR = 4
 F32 = jnp.float32
 BF16 = jnp.bfloat16
 MESH = pl.DeviceIdType.MESH
@@ -99,6 +100,7 @@
     msa_recv,
     upd_send,
     upd_recv,
+    lbuf,
     zbuf,
     rbuf,
     total,
@@ -107,6 +109,8 @@
     msa_rsem,
     upd_ssem,
     upd_rsem,
+    l_ssem,
+    l_rsem,
     z_ssem,
     z_rsem,
     r_ssem,
@@ -118,6 +122,15 @@
     z = lax.div(d, 2)
     xl = lax.rem(d, 2)
     other = 1 - xl
+
+    y, xh, core = lax.div(q, 4), lax.rem(lax.div(q, 2), 2), lax.rem(q, 2)
+    steps = [(2, 1), (1, 1), (3, 1), (2, 0), (0, 1), (1, 0), (3, 0), (0, 0)]
+    partners = [
+        lax.rem(y + a, 4) * 4 + lax.rem(xh + b, 2) * 2 + lax.rem(core + e, 2)
+        for a, b in steps
+        for e in (0, 1)
+        if a + b + e > 0
+    ]
 
     pairs = [
         (x_hbm, x),
@@ -204,9 +217,9 @@
         return jnp.concatenate(tiles, axis=0).reshape(1, 2, 2 * ROWS, LANES).astype(BF16)
 
     zbuf[pl.ds(z, 1)] = fold(right_rows)
-    msa_send[:, 0] = pack_halves(dot(by_residue, normed))
+    msa_send[...] = pack_halves(dot(by_residue, normed))
     left_rows = dot(pick, left_lanes.astype(BF16))
-    msa_send[:, 1:3] = jnp.broadcast_to(fold(left_rows), (GROUPS, 2, 2 * ROWS, LANES))
+    lbuf[pl.ds(q, 1)] = fold(left_rows)
 
     pl.semaphore_wait(barrier, 2 * GROUPS - 1 + z)
 
@@ -232,20 +245,19 @@
     lax.fori_loop(0, z, send_line, 0)
     lax.fori_loop(0, z, answer_line, 0)
 
-    def send_msa(r, _):
-        there = lax.rem(q + r, GROUPS)
-        pltpu.make_async_remote_copy(
-            src_ref=msa_send.at[there],
-            dst_ref=msa_recv.at[q],
-            send_sem=msa_ssem,
-            recv_sem=msa_rsem,
-            device_id=(d, there),
-            device_id_type=MESH,
-        ).start()
-        return 0
-
-    lax.fori_loop(1, GROUPS, send_msa, 0)
-    pltpu.make_async_copy(msa_send.at[q], msa_recv.at[q], msa_rsem).start()
+    def send_rows(out, into, send_sem, recv_sem):
+        for there in partners:
+            pltpu.make_async_remote_copy(
+                src_ref=out.at[there],
+                dst_ref=into.at[q],
+                send_sem=send_sem,
+                recv_sem=recv_sem,
+                device_id=(d, there),
+                device_id_type=MESH,
+            ).start()
+        pltpu.make_async_copy(out.at[q], into.at[q], recv_sem).start()
+
+    send_rows(msa_send, msa_recv, msa_ssem, msa_rsem)
 
     def pass_on(there):
         @pl.when(there != q)
@@ -273,27 +285,68 @@
         ).start()
 
     pass_on(z)
+    for there in partners:
+        pltpu.make_async_remote_copy(
+            src_ref=lbuf.at[q],
+            dst_ref=lbuf.at[q],
+            send_sem=l_ssem,
+            recv_sem=l_rsem,
+            device_id=(d, there),
+            device_id_type=MESH,
+        ).start()
+
+    some = pl.ds(0, GROUPS - 1)
+
+    def sent(ref, sem):
+        pltpu.make_async_copy(ref, ref, sem).wait()
+
+    def take(there):
+        pltpu.make_async_copy(zbuf.at[there], zbuf.at[there], z_rsem.at[there]).wait()
+        pass_on(there)
 
     early = z < EARLY
-
-    def exchange(i, _):
-        there = jnp.where(early, jnp.where(i < EARLY, i, 23 - i), lax.rem(i + EARLY, GROUPS))
-
-        @pl.when(jnp.logical_and(early, there >= EARLY))
+    first = jnp.where(early, 0, EARLY)
+    last = first + EARLY
+
+    def near_send(step, _):
+        @pl.when(z + step < last)
         def _():
-            send_when_ready(there, 0)
-
-        @pl.when(there != z)
+            send_when_ready(z + step, 0)
+
+        return 0
+
+    def near_take(step, _):
+        @pl.when(z + step < last)
         def _():
-            pltpu.make_async_copy(zbuf.at[there], zbuf.at[there], z_rsem.at[there]).wait()
-            pass_on(there)
-
-        return 0
+            take(z + step)
+
+        @pl.when(z - step >= first)
+        def _():
+            take(z - step)
+
+        return 0
+
+    def across(i):
+        return jnp.where(
+            early,
+            jnp.where(z < EARLY // 2, GROUPS - 1 - i, EARLY + i),
+            jnp.where(z < EARLY + EARLY // 2, EARLY - 1 - i, i),
+        )
+
+    def across_send(i, _):
+        return send_when_ready(across(i), 0)
+
+    def across_take(i, _):
+        take(across(i))
+        return 0
+
+    lax.fori_loop(1, NEAR, near_send, 0)
+    lax.fori_loop(1, NEAR, near_take, 0)
 
     for load in loads[7:11]:
         load.wait()
     pltpu.make_async_copy(msa_recv, msa_recv, msa_rsem).wait()
-    items = jnp.concatenate(unpack_halves(msa_recv[:, 0]), axis=1).astype(BF16)
+    items = jnp.concatenate(unpack_halves(msa_recv[...]), axis=1).astype(BF16)
     queries = (dot(items, wq[...]) * HEAD_SIZE ** (-0.5)).astype(BF16)
     keys = dot(items, wk[...]).astype(BF16)
     values = dot(items, wv[...]).astype(BF16)
@@ -319,37 +372,26 @@
     loads[12].wait()
     upd_send[...] = pack_halves(dot(attended, wo[...]) + bo[...])
 
-    def send_update(r, _):
-        there = lax.rem(q + r, GROUPS)
-        pltpu.make_async_remote_copy(
-            src_ref=upd_send.at[there],
-            dst_ref=upd_recv.at[q],
-            send_sem=upd_ssem,
-            recv_sem=upd_rsem,
-            device_id=(d, there),
-            device_id_type=MESH,
-        ).start()
-        return 0
-
-    lax.fori_loop(1, GROUPS, send_update, 0)
-    pltpu.make_async_copy(upd_send.at[q], upd_recv.at[q], upd_rsem).start()
-
-    lax.fori_loop(z + 1, jnp.where(early, EARLY, GROUPS), send_when_ready, 0)
-    lax.fori_loop(0, EARLY, exchange, 0)
+    send_rows(upd_send, upd_recv, upd_ssem, upd_rsem)
+
+    lax.fori_loop(NEAR, EARLY, near_send, 0)
+    lax.fori_loop(0, jnp.where(jnp.logical_and(early, z >= EARLY // 2), EARLY, 0), across_send, 0)
+    lax.fori_loop(NEAR, EARLY, near_take, 0)
+    lax.fori_loop(0, jnp.where(z < EARLY // 2, EARLY, 0), across_send, 0)
+    lax.fori_loop(0, EARLY, across_take, 0)
 
     pltpu.make_async_copy(upd_recv, upd_recv, upd_rsem).wait()
     by_row = (col == lax.rem(row, GROUPS) * ROWS + lax.div(row, GROUPS)).astype(F32).astype(BF16)
     update = jnp.concatenate(unpack_halves(upd_recv[...]), axis=1).astype(BF16)
     column_out[...] = dot(by_row, update).astype(BF16).reshape(ROWS, GROUPS, WIDTH)
 
+    sent(lbuf.at[some], l_rsem)
     left_t = jnp.concatenate(
-        [tile.T for a in (1, 2) for tile in unpack_halves(msa_recv[:, a])], axis=0
+        [tile.T for a in range(2) for tile in unpack_halves(lbuf[:, a])], axis=0
     ).astype(BF16)
     loads[13].wait()
     loads[14].wait()
     kept = jnp.sum(keep)
-
-    lax.fori_loop(EARLY, GROUPS, exchange, 0)
 
     for half in range(2):
         pltpu.make_async_copy(rbuf.at[half], rbuf.at[half], r_rsem.at[half]).wait()
@@ -373,11 +415,7 @@
             (total[half] / kept + bz[...]).astype(BF16).reshape(GROUPS, GROUPS, C_Z)
         )
 
-    some = pl.ds(0, GROUPS - 1)
-
-    def sent(ref, sem):
-        pltpu.make_async_copy(ref, ref, sem).wait()
-
+    sent(lbuf.at[some], l_ssem)
     sent(msa_send.at[some], msa_ssem)
     sent(upd_send.at[some], upd_ssem)
     sent(zbuf.at[some], z_ssem)
@@ -430,10 +468,11 @@
         out_specs=[pl.BlockSpec(memory_space=pltpu.VMEM)] * 2,
         scratch_shapes=[pltpu.VMEM(a.shape, a.dtype) for a in args]
         + [
-            pltpu.VMEM((GROUPS, 3, *piece), BF16),
-            pltpu.VMEM((GROUPS, 3, *piece), BF16),
             pltpu.VMEM((GROUPS, *piece), BF16),
             pltpu.VMEM((GROUPS, *piece), BF16),
+            pltpu.VMEM((GROUPS, *piece), BF16),
+            pltpu.VMEM((GROUPS, *piece), BF16),
+            pltpu.VMEM((GROUPS, 2, *piece), BF16),
             pltpu.VMEM((GROUPS, 2, *piece), BF16),
             pltpu.VMEM((2, GROUPS, 2, *piece), BF16),
             pltpu.VMEM((2, WIDTH, C_Z), F32),
@@ -443,16 +482,18 @@
             pltpu.SemaphoreType.DMA,
             pltpu.SemaphoreType.DMA,
             pltpu.SemaphoreType.DMA,
+            pltpu.SemaphoreType.DMA,
+            pltpu.SemaphoreType.DMA,
             pltpu.SemaphoreType.DMA((GROUPS,)),
             pltpu.SemaphoreType.DMA,
             pltpu.SemaphoreType.DMA((2,)),
             pltpu.SemaphoreType.REGULAR((GROUPS,)),
         ],
         compiler_params=pltpu.CompilerParams(
-            collective_id=0, has_side_effects=True, vmem_limit_bytes=60 * 1024 * 1024
+            collective_id=0, has_side_effects=True, vmem_limit_bytes=16 * 1024 * 1024
         ),
         name="column_attention_and_outer_mean",
-    )(*args)
+    )(*[pltpu.with_memory_space_constraint(a, pltpu.HBM) for a in args])
 
 
 def solution(mesh):

time: 36.4 us -> 31 us (0.85)
  the two profiles are of different devices: /device:TPU:393 before, /device:TPU:481 now
where the time goes in v3:
time: 31 us; the launch traced here: 30.9 us
  Pallas kernels  28.9 us (93%)
  local copies, waits for them, and re-layouts  1.29 us (4%)
  between operations  0.64 us (2%)
    pallas_call x1, Pallas kernels, local(): pl.pallas_call(kernel, out_shape=(jax.ShapeDtypeStruct((ROWS, GROUPS, WID...  28.9 us
    unnamed x2, local copies, waits for them, and re-layouts  1.29 us

profile of v3, /device:TPU:481, one launch (start us, length us, event | category | flops | bytes accessed | tf_op | source)
XLA Modules:
  0.0 30.9 jit_solution(11585174452912448834)
XLA Ops:
  0.6 28.9 %column_attention_and_outer_mean.1 = (bf16[8,16,256]{2,1,0:T(8,128)(2,1)S(1)}, bf16[16,32,128]{2,1,0:T(8,128)(2,1)S(1)}) custom-call(bf16[8,16,256]{2,1,0:T(8,128)(2,1)} %x_hbm.1, s32[1,128]{1,0:T(1,128)} %bitcast.12, s32[1,512]{1,0:T(1,128)} %bitcast.10, bf16[256,256]{1,0:T(8,128)(2,1)} %wq_hbm.1, bf16[256,256]{1,0:T(8,128)(2,1)} %wk_hbm.1, ...), custom_call_target="tpu_custom_call" | custom-call | tf_op jit(solution)/shard_map/column_attention_and_outer_mean/pallas_call | solution.py:461
  29.6 0.6 %copy.19 = bf16[8,16,256]{2,1,0:T(8,128)(2,1)} copy(bf16[8,16,256]{2,1,0:T(8,128)(2,1)S(1)} %get-tuple-element.4) | data formatting | bytes 131072
  30.2 0.7 %copy.20 = bf16[16,32,128]{2,1,0:T(8,128)(2,1)} copy(bf16[16,32,128]{2,1,0:T(8,128)(2,1)S(1)} %get-tuple-element.5) | data formatting | bytes 262144

commit v4 on v3

--- a/solution.py
+++ b/solution.py
@@ -14,8 +14,8 @@
 HEAD_SIZE = 32
 FACTORS = 32
 C_Z = 128
-EARLY = 8
-NEAR = 4
+BLOCK = 8
+REACH = 4
 F32 = jnp.float32
 BF16 = jnp.bfloat16
 MESH = pl.DeviceIdType.MESH
@@ -111,7 +111,9 @@
     upd_rsem,
     l_ssem,
     l_rsem,
-    z_ssem,
+    across_ssem,
+    near_ssem,
+    relay_ssem,
     z_rsem,
     r_ssem,
     r_rsem,
@@ -122,15 +124,6 @@
     z = lax.div(d, 2)
     xl = lax.rem(d, 2)
     other = 1 - xl
-
-    y, xh, core = lax.div(q, 4), lax.rem(lax.div(q, 2), 2), lax.rem(q, 2)
-    steps = [(2, 1), (1, 1), (3, 1), (2, 0), (0, 1), (1, 0), (3, 0), (0, 0)]
-    partners = [
-        lax.rem(y + a, 4) * 4 + lax.rem(xh + b, 2) * 2 + lax.rem(core + e, 2)
-        for a, b in steps
-        for e in (0, 1)
-        if a + b + e > 0
-    ]
 
     pairs = [
         (x_hbm, x),
@@ -150,30 +143,48 @@
         (bz_hbm, bz),
     ]
     loads = [pltpu.make_async_copy(a, b, load_sem.at[i]) for i, (a, b) in enumerate(pairs)]
-    for load in loads:
-        load.start()
+    loads[0].start()
+
+    y, xh, core = lax.div(q, 4), lax.rem(lax.div(q, 2), 2), lax.rem(q, 2)
+    steps = [(2, 1), (1, 1), (3, 1), (2, 0), (0, 1), (1, 0), (3, 0), (0, 0)]
+    partners = [
+        lax.rem(y + a, 4) * 4 + lax.rem(xh + b, 2) * 2 + lax.rem(core + e, 2)
+        for a, b in steps
+        for e in (0, 1)
+        if a + b + e > 0
+    ]
 
     barrier = pltpu.get_barrier_semaphore()
 
     def line(there):
         return (there * 2 + xl, q)
 
+    early = z < BLOCK
+    first = jnp.where(early, 0, BLOCK)
+    last = first + BLOCK
+    reach = jnp.where(early, BLOCK, REACH)
+    reach_low = jnp.maximum(z - reach, first)
+    reach_high = jnp.minimum(z + reach + 1, last)
+    before = jnp.where(early, REACH - 1, REACH)
+    before_high = jnp.minimum(z + before + 1, last)
+    below = jnp.where(early, 0, BLOCK)
+
     def greet_line(there, _):
         pl.semaphore_signal(barrier, inc=1, device_id=line(there), device_id_type=MESH)
         return 0
 
-    def greet_plane(r, _):
-        there = lax.rem(xl * GROUPS + q + r, 2 * GROUPS)
-        pl.semaphore_signal(
-            barrier,
-            inc=1,
-            device_id=(z * 2 + lax.div(there, GROUPS), lax.rem(there, GROUPS)),
-            device_id_type=MESH,
-        )
-        return 0
-
-    lax.fori_loop(1, 2 * GROUPS, greet_plane, 0)
-    lax.fori_loop(z + 1, GROUPS, greet_line, 0)
+    def greet(there_d, there_q):
+        pl.semaphore_signal(barrier, inc=1, device_id=(there_d, there_q), device_id_type=MESH)
+
+    lax.fori_loop(z + 1, reach_high, greet_line, 0)
+    lax.fori_loop(BLOCK, BLOCK + BLOCK - below, greet_line, 0)
+    for there in partners:
+        greet(z * 2 + other, there)
+        greet(d, there)
+    greet(z * 2 + other, q)
+
+    for load in loads[1:]:
+        load.start()
 
     loads[0].wait()
     wide = x[...].astype(F32).reshape(TOKENS, WIDTH)
@@ -221,29 +232,34 @@
     left_rows = dot(pick, left_lanes.astype(BF16))
     lbuf[pl.ds(q, 1)] = fold(left_rows)
 
-    pl.semaphore_wait(barrier, 2 * GROUPS - 1 + z)
-
-    def send_line(there, _):
+    pl.semaphore_wait(barrier, 2 * GROUPS - 1 + z - reach_low + below)
+
+    def send_piece(piece, there, sem):
         pltpu.make_async_remote_copy(
-            src_ref=zbuf.at[z],
-            dst_ref=zbuf.at[z],
-            send_sem=z_ssem,
-            recv_sem=z_rsem.at[z],
+            src_ref=zbuf.at[piece],
+            dst_ref=zbuf.at[piece],
+            send_sem=sem,
+            recv_sem=z_rsem.at[piece],
             device_id=line(there),
             device_id_type=MESH,
         ).start()
+
+    def send_across(there, _):
+        send_piece(z, there, across_ssem)
+        return 0
+
+    def send_near(there, _):
+        send_piece(z, there, near_ssem.at[there])
         return 0
 
     def answer_line(there, _):
         pl.semaphore_signal(ready.at[z], inc=1, device_id=line(there), device_id_type=MESH)
         return 0
 
-    def send_when_ready(there, _):
-        pl.semaphore_wait(ready.at[there], 1)
-        return send_line(there, 0)
-
-    lax.fori_loop(0, z, send_line, 0)
-    lax.fori_loop(0, z, answer_line, 0)
+    lax.fori_loop(0, below, send_across, 0)
+    lax.fori_loop(reach_low, z, send_near, 0)
+    lax.fori_loop(0, below, answer_line, 0)
+    lax.fori_loop(reach_low, z, answer_line, 0)
 
     def send_rows(out, into, send_sem, recv_sem):
         for there in partners:
@@ -285,15 +301,6 @@
         ).start()
 
     pass_on(z)
-    for there in partners:
-        pltpu.make_async_remote_copy(
-            src_ref=lbuf.at[q],
-            dst_ref=lbuf.at[q],
-            send_sem=l_ssem,
-            recv_sem=l_rsem,
-            device_id=(d, there),
-            device_id_type=MESH,
-        ).start()
 
     some = pl.ds(0, GROUPS - 1)
 
@@ -304,16 +311,9 @@
         pltpu.make_async_copy(zbuf.at[there], zbuf.at[there], z_rsem.at[there]).wait()
         pass_on(there)
 
-    early = z < EARLY
-    first = jnp.where(early, 0, EARLY)
-    last = first + EARLY
-
-    def near_send(step, _):
-        @pl.when(z + step < last)
-        def _():
-            send_when_ready(z + step, 0)
-
-        return 0
+    def near_send(there, _):
+        pl.semaphore_wait(ready.at[there], 1)
+        return send_near(there, 0)
 
     def near_take(step, _):
         @pl.when(z + step < last)
@@ -325,23 +325,38 @@
             take(z - step)
 
         return 0
+
+    def relay(away):
+        piece = z + away
+
+        @pl.when(jnp.logical_and(jnp.logical_not(early), jnp.logical_and(piece >= first, piece < last)))
+        def _():
+            take(piece)
+            for i in range(1, REACH):
+                there = z - i if away > 0 else z + i
+
+                @pl.when(jnp.logical_and(there >= first, there < last))
+                def _():
+                    send_piece(piece, there, relay_ssem.at[i])
 
     def across(i):
         return jnp.where(
             early,
-            jnp.where(z < EARLY // 2, GROUPS - 1 - i, EARLY + i),
-            jnp.where(z < EARLY + EARLY // 2, EARLY - 1 - i, i),
+            jnp.where(z < BLOCK // 2, GROUPS - 1 - i, BLOCK + i),
+            jnp.where(z < BLOCK + BLOCK // 2, BLOCK - 1 - i, i),
         )
 
     def across_send(i, _):
-        return send_when_ready(across(i), 0)
+        there = across(i)
+        pl.semaphore_wait(ready.at[there], 1)
+        return send_across(there, 0)
 
     def across_take(i, _):
         take(across(i))
         return 0
 
-    lax.fori_loop(1, NEAR, near_send, 0)
-    lax.fori_loop(1, NEAR, near_take, 0)
+    lax.fori_loop(z + 1, before_high, near_send, 0)
+    lax.fori_loop(1, REACH, near_take, 0)
 
     for load in loads[7:11]:
         load.wait()
@@ -373,12 +388,23 @@
     upd_send[...] = pack_halves(dot(attended, wo[...]) + bo[...])
 
     send_rows(upd_send, upd_recv, upd_ssem, upd_rsem)
-
-    lax.fori_loop(NEAR, EARLY, near_send, 0)
-    lax.fori_loop(0, jnp.where(jnp.logical_and(early, z >= EARLY // 2), EARLY, 0), across_send, 0)
-    lax.fori_loop(NEAR, EARLY, near_take, 0)
-    lax.fori_loop(0, jnp.where(z < EARLY // 2, EARLY, 0), across_send, 0)
-    lax.fori_loop(0, EARLY, across_take, 0)
+    for there in partners:
+        pltpu.make_async_remote_copy(
+            src_ref=lbuf.at[q],
+            dst_ref=lbuf.at[q],
+            send_sem=l_ssem,
+            recv_sem=l_rsem,
+            device_id=(d, there),
+            device_id_type=MESH,
+        ).start()
+
+    relay(REACH)
+    relay(-REACH)
+    lax.fori_loop(before_high, reach_high, near_send, 0)
+    lax.fori_loop(0, jnp.where(jnp.logical_and(early, z >= BLOCK // 2), BLOCK, 0), across_send, 0)
+    lax.fori_loop(before + 1, BLOCK, near_take, 0)
+    lax.fori_loop(0, jnp.where(z < BLOCK // 2, BLOCK, 0), across_send, 0)
+    lax.fori_loop(0, BLOCK, across_take, 0)
 
     pltpu.make_async_copy(upd_recv, upd_recv, upd_rsem).wait()
     by_row = (col == lax.rem(row, GROUPS) * ROWS + lax.div(row, GROUPS)).astype(F32).astype(BF16)
@@ -398,7 +424,7 @@
         rights = jnp.concatenate(
             [tile for a in range(2) for tile in unpack_halves(rbuf[half, :, a])], axis=1
         ).astype(BF16)
-        outer = dot(left_t, rights).reshape(FACTORS, GROUPS, 4 * LANES)
+        outer = dot(left_t, rights).astype(BF16).reshape(FACTORS, GROUPS, 4 * LANES)
         rows = [[None] * 8 for _ in range(GROUPS)]
         for c in range(8):
             for j in range(4):
@@ -406,7 +432,7 @@
                     [outer[4 * c + a, :, LANES * j : LANES * (j + 1)] for a in range(4)]
                 )
                 for b in range(4):
-                    rows[4 * j + b][c] = moved[b].astype(BF16)
+                    rows[4 * j + b][c] = moved[b]
         flat = jnp.concatenate([jnp.concatenate(r, axis=1) for r in rows], axis=0)
         sums = dot(flat, wz[...])
         for k in range(GROUPS):
@@ -418,9 +444,37 @@
     sent(lbuf.at[some], l_ssem)
     sent(msa_send.at[some], msa_ssem)
     sent(upd_send.at[some], upd_ssem)
-    sent(zbuf.at[some], z_ssem)
+    sent(zbuf.at[pl.ds(0, BLOCK)], across_ssem)
+
+    def near_sent(there, _):
+        @pl.when(there != z)
+        def _():
+            sent(zbuf.at[0], near_ssem.at[there])
+
+        return 0
+
+    lax.fori_loop(reach_low, reach_high, near_sent, 0)
+    for i in range(1, REACH):
+        up = jnp.logical_and(z - REACH >= first, z + i < last)
+        down = jnp.logical_and(z + REACH < last, z - i >= first)
+
+        @pl.when(jnp.logical_and(jnp.logical_not(early), jnp.logical_or(up, down)))
+        def _():
+            sent(zbuf.at[0], relay_ssem.at[i])
+
     sent(zbuf, r_ssem)
     sent(zbuf.at[some], r_ssem)
+
+
+def store(column, pair, column_out, pair_out, sem):
+    copies = [
+        pltpu.make_async_copy(pair, pair_out, sem.at[0]),
+        pltpu.make_async_copy(column, column_out, sem.at[1]),
+    ]
+    for copy in copies:
+        copy.start()
+    for copy in copies:
+        copy.wait()
 
 
 def local(
@@ -458,7 +512,7 @@
         couple_change_offset.reshape(1, -1),
     )
     piece = (2 * ROWS, LANES)
-    return pl.pallas_call(
+    results = pl.pallas_call(
         kernel,
         out_shape=(
             jax.ShapeDtypeStruct((ROWS, GROUPS, WIDTH), BF16),
@@ -485,6 +539,8 @@
             pltpu.SemaphoreType.DMA,
             pltpu.SemaphoreType.DMA,
             pltpu.SemaphoreType.DMA((GROUPS,)),
+            pltpu.SemaphoreType.DMA((REACH,)),
+            pltpu.SemaphoreType.DMA((GROUPS,)),
             pltpu.SemaphoreType.DMA,
             pltpu.SemaphoreType.DMA((2,)),
             pltpu.SemaphoreType.REGULAR((GROUPS,)),
@@ -494,6 +550,15 @@
         ),
         name="column_attention_and_outer_mean",
     )(*[pltpu.with_memory_space_constraint(a, pltpu.HBM) for a in args])
+    return pl.pallas_call(
+        store,
+        out_shape=tuple(jax.ShapeDtypeStruct(r.shape, r.dtype) for r in results),
+        in_specs=[pl.BlockSpec(memory_space=pltpu.VMEM)] * 2,
+        out_specs=[pl.BlockSpec(memory_space=pltpu.HBM)] * 2,
+        scratch_shapes=[pltpu.SemaphoreType.DMA((2,))],
+        compiler_params=pltpu.CompilerParams(vmem_limit_bytes=2 * 1024 * 1024),
+        name="store_results",
+    )(*[pltpu.with_memory_space_constraint(r, pltpu.VMEM) for r in results])
 
 
 def solution(mesh):

time: 31 us -> 29.3 us (0.945)
  the two profiles are of different devices: /device:TPU:481 before, /device:TPU:48 now
where the time goes in v4:
time: 29.3 us; the launch traced here: 29.1 us
  Pallas kernels  28.4 us (97%)
  between operations  0.64 us (2%)
    pallas_call x1, Pallas kernels, local(): pl.pallas_call(kernel, out_shape=(jax.ShapeDtypeStruct((ROWS, GROUPS, WID...  27.8 us
    pallas_call x1, Pallas kernels, local(): pl.pallas_call(store, out_shape=tuple((jax.ShapeDtypeStruct(r.shape, r.dt...  0.69 us

profile of v4, /device:TPU:48, one launch (start us, length us, event | category | flops | bytes accessed | tf_op | source)
XLA Modules:
  0.0 29.1 jit_solution(1911998263882068586)
XLA Ops:
  0.6 27.8 %column_attention_and_outer_mean.1 = (bf16[8,16,256]{2,1,0:T(8,128)(2,1)S(1)}, bf16[16,32,128]{2,1,0:T(8,128)(2,1)S(1)}) custom-call(bf16[8,16,256]{2,1,0:T(8,128)(2,1)} %x_hbm.1, s32[1,128]{1,0:T(1,128)} %bitcast.12, s32[1,512]{1,0:T(1,128)} %bitcast.10, bf16[256,256]{1,0:T(8,128)(2,1)} %wq_hbm.1, bf16[256,256]{1,0:T(8,128)(2,1)} %wk_hbm.1, ...), custom_call_target="tpu_custom_call" | custom-call | tf_op jit(solution)/shard_map/column_attention_and_outer_mean/pallas_call | solution.py:515
  28.4 0.7 %store_results.1 = (bf16[8,16,256]{2,1,0:T(8,128)(2,1)}, bf16[16,32,128]{2,1,0:T(8,128)(2,1)}) custom-call(bf16[8,16,256]{2,1,0:T(8,128)(2,1)S(1)} %get-tuple-element.4.column, bf16[16,32,128]{2,1,0:T(8,128)(2,1)S(1)} %get-tuple-element.5.pair), custom_call_target="tpu_custom_call" | custom-call | tf_op jit(solution)/shard_map/store_results/pallas_call | solution.py:553

commit v5 on v4

--- a/solution.py
+++ b/solution.py
@@ -15,6 +15,7 @@
 FACTORS = 32
 C_Z = 128
 BLOCK = 8
+QUAD = 4
 REACH = 4
 F32 = jnp.float32
 BF16 = jnp.bfloat16
@@ -45,22 +46,6 @@
         tall[:, :ROWS].reshape(TOKENS, LANES),
         tall[:, ROWS:].reshape(TOKENS, LANES),
     )
-
-
-def swap_blocks(v):
-    block = iota(v[0].shape, v[0].ndim - 1) // FACTORS
-    odd = block % 2 == 1
-    high = block >= 2
-    axis = v[0].ndim - 1
-    u = [None] * 4
-    for a in (0, 2):
-        u[a] = jnp.where(odd, pltpu.roll(v[a + 1], 32, axis), v[a])
-        u[a + 1] = jnp.where(odd, v[a + 1], pltpu.roll(v[a], 96, axis))
-    w = [None] * 4
-    for a in (0, 1):
-        w[a] = jnp.where(high, pltpu.roll(u[a + 2], 64, axis), u[a])
-        w[a + 2] = jnp.where(high, u[a + 2], pltpu.roll(u[a], 64, axis))
-    return w
 
 
 def kernel(
@@ -112,6 +97,7 @@
     l_ssem,
     l_rsem,
     across_ssem,
+    far_ssem,
     near_ssem,
     relay_ssem,
     z_rsem,
@@ -159,6 +145,7 @@
     def line(there):
         return (there * 2 + xl, q)
 
+    quad = lax.div(z, QUAD)
     early = z < BLOCK
     first = jnp.where(early, 0, BLOCK)
     last = first + BLOCK
@@ -256,7 +243,7 @@
         pl.semaphore_signal(ready.at[z], inc=1, device_id=line(there), device_id_type=MESH)
         return 0
 
-    lax.fori_loop(0, below, send_across, 0)
+    lax.fori_loop(0, jnp.where(quad == 3, QUAD, below), send_across, 0)
     lax.fori_loop(reach_low, z, send_near, 0)
     lax.fori_loop(0, below, answer_line, 0)
     lax.fori_loop(reach_low, z, answer_line, 0)
@@ -339,23 +326,40 @@
                 def _():
                     send_piece(piece, there, relay_ssem.at[i])
 
-    def across(i):
-        return jnp.where(
-            early,
-            jnp.where(z < BLOCK // 2, GROUPS - 1 - i, BLOCK + i),
-            jnp.where(z < BLOCK + BLOCK // 2, BLOCK - 1 - i, i),
-        )
-
     def across_send(i, _):
-        there = across(i)
+        there = jnp.where(quad == 0, GROUPS - 1 - i, BLOCK + i)
         pl.semaphore_wait(ready.at[there], 1)
         return send_across(there, 0)
 
     def across_take(i, _):
-        take(across(i))
+        here = i < QUAD
+        piece = jnp.where(
+            early,
+            jnp.where(
+                quad == 0,
+                jnp.where(jnp.logical_or(here, z < 2), GROUPS - 1 - i, QUAD + i),
+                BLOCK + i,
+            ),
+            jnp.where(quad == 2, BLOCK - 1 - i, i),
+        )
+        take(piece)
+
+        @pl.when(jnp.logical_and(here, quad == 0))
+        def _():
+            send_piece(piece, z + QUAD, far_ssem)
+
         return 0
 
     lax.fori_loop(z + 1, before_high, near_send, 0)
+    for there in partners:
+        pltpu.make_async_remote_copy(
+            src_ref=lbuf.at[q],
+            dst_ref=lbuf.at[q],
+            send_sem=l_ssem,
+            recv_sem=l_rsem,
+            device_id=(d, there),
+            device_id_type=MESH,
+        ).start()
     lax.fori_loop(1, REACH, near_take, 0)
 
     for load in loads[7:11]:
@@ -387,23 +391,13 @@
     loads[12].wait()
     upd_send[...] = pack_halves(dot(attended, wo[...]) + bo[...])
 
-    send_rows(upd_send, upd_recv, upd_ssem, upd_rsem)
-    for there in partners:
-        pltpu.make_async_remote_copy(
-            src_ref=lbuf.at[q],
-            dst_ref=lbuf.at[q],
-            send_sem=l_ssem,
-            recv_sem=l_rsem,
-            device_id=(d, there),
-            device_id_type=MESH,
-        ).start()
-
     relay(REACH)
     relay(-REACH)
     lax.fori_loop(before_high, reach_high, near_send, 0)
-    lax.fori_loop(0, jnp.where(jnp.logical_and(early, z >= BLOCK // 2), BLOCK, 0), across_send, 0)
+    lax.fori_loop(0, jnp.where(quad == 1, BLOCK, 0), across_send, 0)
+    send_rows(upd_send, upd_recv, upd_ssem, upd_rsem)
     lax.fori_loop(before + 1, BLOCK, near_take, 0)
-    lax.fori_loop(0, jnp.where(z < BLOCK // 2, BLOCK, 0), across_send, 0)
+    lax.fori_loop(0, jnp.where(quad == 0, BLOCK, 0), across_send, 0)
     lax.fori_loop(0, BLOCK, across_take, 0)
 
     pltpu.make_async_copy(upd_recv, upd_recv, upd_rsem).wait()
@@ -412,39 +406,92 @@
     column_out[...] = dot(by_row, update).astype(BF16).reshape(ROWS, GROUPS, WIDTH)
 
     sent(lbuf.at[some], l_rsem)
-    left_t = jnp.concatenate(
-        [tile.T for a in range(2) for tile in unpack_halves(lbuf[:, a])], axis=0
-    ).astype(BF16)
+    gap = jnp.zeros((GROUPS, ROWS, LANES), F32)
+    lefts = []
+    for side in range(2):
+        parts = []
+        for a in range(2):
+            for tile in unpack_halves(lbuf[:, a]):
+                rows = [tile.reshape(GROUPS, ROWS, LANES), gap]
+                parts.append(
+                    jnp.concatenate(rows[::-1] if side else rows, axis=1)
+                    .reshape(2 * TOKENS, LANES)
+                    .T
+                )
+        lefts.append(
+            jnp.concatenate(parts, axis=0).astype(BF16).reshape(8, 4, GROUPS, 2 * TOKENS)
+        )
     loads[13].wait()
     loads[14].wait()
     kept = jnp.sum(keep)
 
     for half in range(2):
         pltpu.make_async_copy(rbuf.at[half], rbuf.at[half], r_rsem.at[half]).wait()
-        rights = jnp.concatenate(
-            [tile for a in range(2) for tile in unpack_halves(rbuf[half, :, a])], axis=1
-        ).astype(BF16)
-        outer = dot(left_t, rights).astype(BF16).reshape(FACTORS, GROUPS, 4 * LANES)
-        rows = [[None] * 8 for _ in range(GROUPS)]
-        for c in range(8):
-            for j in range(4):
-                moved = swap_blocks(
-                    [outer[4 * c + a, :, LANES * j : LANES * (j + 1)] for a in range(4)]
-                )
-                for b in range(4):
-                    rows[4 * j + b][c] = moved[b]
-        flat = jnp.concatenate([jnp.concatenate(r, axis=1) for r in rows], axis=0)
-        sums = dot(flat, wz[...])
-        for k in range(GROUPS):
-            total[half, pl.ds(k, GROUPS, stride=GROUPS), :] = sums[GROUPS * k : GROUPS * (k + 1)]
-        pair_out[:, half * GROUPS : (half + 1) * GROUPS, :] = (
-            (total[half] / kept + bz[...]).astype(BF16).reshape(GROUPS, GROUPS, C_Z)
+    right = jnp.concatenate(
+        [rbuf[half, :, a].reshape(2 * TOKENS, LANES) for half in range(2) for a in range(2)], axis=1
+    )
+
+    products = []
+    for a in range(4):
+        turned = [
+            right[:, LANES * t : LANES * (t + 1)]
+            if a == 0
+            else pltpu.roll(right[:, LANES * t : LANES * (t + 1)], FACTORS * a, 1)
+            for t in range(4)
+        ]
+        turned = jnp.concatenate(turned, axis=1)
+        products.append(
+            [
+                dot(lefts[side][:, a].reshape(TOKENS, 2 * TOKENS), turned)
+                .astype(BF16)
+                .reshape(8, GROUPS, 4 * LANES)
+                for side in range(2)
+            ]
         )
+
+    block = lax.div(iota((GROUPS, LANES), 1), FACTORS)
+    odd, high = lax.rem(block, 2) == 1, block >= 2
+    flat = [[[None] * 8 for _ in range(8)] for _ in range(4)]
+    for t in range(4):
+        for side in range(2):
+            for c in range(8):
+                v = [products[a][side][c, :, LANES * t : LANES * (t + 1)] for a in range(4)]
+                even_up, even_down = jnp.where(high, v[2], v[0]), jnp.where(high, v[0], v[2])
+                odd_up, odd_down = jnp.where(high, v[3], v[1]), jnp.where(high, v[1], v[3])
+                place = 2 * t + side
+                flat[0][place][c] = jnp.where(odd, odd_up, even_up)
+                flat[1][place][c] = jnp.where(odd, even_up, odd_down)
+                flat[2][place][c] = jnp.where(odd, odd_down, even_down)
+                flat[3][place][c] = jnp.where(odd, even_down, odd_up)
+    couple = wz[...].reshape(8, 4, FACTORS, C_Z)
+    for b in range(4):
+        mixing = jnp.concatenate(
+            [couple[c, (g - b) % 4] for c in range(8) for g in range(4)], axis=0
+        )
+        sums = dot(
+            jnp.concatenate([jnp.concatenate(r, axis=1) for r in flat[b]], axis=0), mixing
+        )
+        for place in range(8):
+            total[pl.ds(4 * place + b, GROUPS, stride=2 * GROUPS), :] = sums[
+                GROUPS * place : GROUPS * (place + 1)
+            ]
+    pair_out[...] = (total[...] / kept + bz[...]).astype(BF16).reshape(GROUPS, 2 * GROUPS, C_Z)
 
     sent(lbuf.at[some], l_ssem)
     sent(msa_send.at[some], msa_ssem)
     sent(upd_send.at[some], upd_ssem)
-    sent(zbuf.at[pl.ds(0, BLOCK)], across_ssem)
+
+    @pl.when(quad == 3)
+    def _():
+        sent(zbuf.at[pl.ds(0, QUAD)], across_ssem)
+
+    @pl.when(quad != 3)
+    def _():
+        sent(zbuf.at[pl.ds(0, BLOCK)], across_ssem)
+
+    @pl.when(quad == 0)
+    def _():
+        sent(zbuf.at[pl.ds(0, QUAD)], far_ssem)
 
     def near_sent(there, _):
         @pl.when(there != z)
@@ -529,8 +576,9 @@
             pltpu.VMEM((GROUPS, 2, *piece), BF16),
             pltpu.VMEM((GROUPS, 2, *piece), BF16),
             pltpu.VMEM((2, GROUPS, 2, *piece), BF16),
-            pltpu.VMEM((2, WIDTH, C_Z), F32),
+            pltpu.VMEM((2 * WIDTH, C_Z), F32),
             pltpu.SemaphoreType.DMA((len(args),)),
+            pltpu.SemaphoreType.DMA,
             pltpu.SemaphoreType.DMA,
             pltpu.SemaphoreType.DMA,
             pltpu.SemaphoreType.DMA,

time: 29.3 us -> 28.4 us (0.969)
  the two profiles are of different devices: /device:TPU:48 before, /device:TPU:49 now
where the time goes in v5:
time: 28.4 us; the launch traced here: 28.3 us
  Pallas kernels  27.6 us (97%)
  between operations  0.64 us (2%)
    pallas_call x1, Pallas kernels, local(): pl.pallas_call(kernel, out_shape=(jax.ShapeDtypeStruct((ROWS, GROUPS, WID...  26.9 us
    pallas_call x1, Pallas kernels, local(): pl.pallas_call(store, out_shape=tuple((jax.ShapeDtypeStruct(r.shape, r.dt...  0.69 us

profile of v5, /device:TPU:49, one launch (start us, length us, event | category | flops | bytes accessed | tf_op | source)
XLA Modules:
  0.0 28.3 jit_solution(10686070064260204318)
XLA Ops:
  0.6 26.9 %column_attention_and_outer_mean.1 = (bf16[8,16,256]{2,1,0:T(8,128)(2,1)S(1)}, bf16[16,32,128]{2,1,0:T(8,128)(2,1)S(1)}) custom-call(bf16[8,16,256]{2,1,0:T(8,128)(2,1)} %x_hbm.1, s32[1,128]{1,0:T(1,128)} %bitcast.12, s32[1,512]{1,0:T(1,128)} %bitcast.10, bf16[256,256]{1,0:T(8,128)(2,1)} %wq_hbm.1, bf16[256,256]{1,0:T(8,128)(2,1)} %wk_hbm.1, ...), custom_call_target="tpu_custom_call" | custom-call | tf_op jit(solution)/shard_map/column_attention_and_outer_mean/pallas_call | solution.py:562
  27.6 0.7 %store_results.1 = (bf16[8,16,256]{2,1,0:T(8,128)(2,1)}, bf16[16,32,128]{2,1,0:T(8,128)(2,1)}) custom-call(bf16[8,16,256]{2,1,0:T(8,128)(2,1)S(1)} %get-tuple-element.4.column, bf16[16,32,128]{2,1,0:T(8,128)(2,1)S(1)} %get-tuple-element.5.pair), custom_call_target="tpu_custom_call" | custom-call | tf_op jit(solution)/shard_map/store_results/pallas_call | solution.py:601

commit v6 on v5

--- a/solution.py
+++ b/solution.py
@@ -16,6 +16,7 @@
 C_Z = 128
 BLOCK = 8
 QUAD = 4
+SOON = 6
 REACH = 4
 F32 = jnp.float32
 BF16 = jnp.bfloat16
@@ -243,7 +244,10 @@
         pl.semaphore_signal(ready.at[z], inc=1, device_id=line(there), device_id_type=MESH)
         return 0
 
-    lax.fori_loop(0, jnp.where(quad == 3, QUAD, below), send_across, 0)
+    def send_far_first(i, _):
+        return send_across(i, 0)
+
+    lax.fori_loop(0, jnp.where(early, 0, QUAD), send_far_first, 0)
     lax.fori_loop(reach_low, z, send_near, 0)
     lax.fori_loop(0, below, answer_line, 0)
     lax.fori_loop(reach_low, z, answer_line, 0)
@@ -350,17 +354,12 @@
 
         return 0
 
+    lax.fori_loop(QUAD, jnp.where(quad == 2, BLOCK, QUAD), send_far_first, 0)
     lax.fori_loop(z + 1, before_high, near_send, 0)
-    for there in partners:
-        pltpu.make_async_remote_copy(
-            src_ref=lbuf.at[q],
-            dst_ref=lbuf.at[q],
-            send_sem=l_ssem,
-            recv_sem=l_rsem,
-            device_id=(d, there),
-            device_id_type=MESH,
-        ).start()
     lax.fori_loop(1, REACH, near_take, 0)
+
+    soon = jnp.where(jnp.logical_and(early, z >= SOON), QUAD, 0)
+    lax.fori_loop(0, soon, across_send, 0)
 
     for load in loads[7:11]:
         load.wait()
@@ -394,8 +393,17 @@
     relay(REACH)
     relay(-REACH)
     lax.fori_loop(before_high, reach_high, near_send, 0)
-    lax.fori_loop(0, jnp.where(quad == 1, BLOCK, 0), across_send, 0)
+    lax.fori_loop(soon, jnp.where(quad == 1, BLOCK, 0), across_send, 0)
     send_rows(upd_send, upd_recv, upd_ssem, upd_rsem)
+    for there in partners:
+        pltpu.make_async_remote_copy(
+            src_ref=lbuf.at[q],
+            dst_ref=lbuf.at[q],
+            send_sem=l_ssem,
+            recv_sem=l_rsem,
+            device_id=(d, there),
+            device_id_type=MESH,
+        ).start()
     lax.fori_loop(before + 1, BLOCK, near_take, 0)
     lax.fori_loop(0, jnp.where(quad == 0, BLOCK, 0), across_send, 0)
     lax.fori_loop(0, BLOCK, across_take, 0)

time: 28.4 us -> 28.3 us (level)
  the two profiles are of different devices: /device:TPU:49 before, /device:TPU:249 now
where the time goes in v6:
time: 28.3 us; the launch traced here: 28.1 us
  Pallas kernels  27.5 us (97%)
  between operations  0.64 us (2%)
    pallas_call x1, Pallas kernels, local(): pl.pallas_call(kernel, out_shape=(jax.ShapeDtypeStruct((ROWS, GROUPS, WID...  26.8 us
    pallas_call x1, Pallas kernels, local(): pl.pallas_call(store, out_shape=tuple((jax.ShapeDtypeStruct(r.shape, r.dt...  0.69 us

profile of v6, /device:TPU:249, one launch (start us, length us, event | category | flops | bytes accessed | tf_op | source)
XLA Modules:
  0.0 28.1 jit_solution(17279023557991088150)
XLA Ops:
  0.6 26.8 %column_attention_and_outer_mean.1 = (bf16[8,16,256]{2,1,0:T(8,128)(2,1)S(1)}, bf16[16,32,128]{2,1,0:T(8,128)(2,1)S(1)}) custom-call(bf16[8,16,256]{2,1,0:T(8,128)(2,1)} %x_hbm.1, s32[1,128]{1,0:T(1,128)} %bitcast.12, s32[1,512]{1,0:T(1,128)} %bitcast.10, bf16[256,256]{1,0:T(8,128)(2,1)} %wq_hbm.1, bf16[256,256]{1,0:T(8,128)(2,1)} %wk_hbm.1, ...), custom_call_target="tpu_custom_call" | custom-call | tf_op jit(solution)/shard_map/column_attention_and_outer_mean/pallas_call | solution.py:570
  27.4 0.7 %store_results.1 = (bf16[8,16,256]{2,1,0:T(8,128)(2,1)}, bf16[16,32,128]{2,1,0:T(8,128)(2,1)}) custom-call(bf16[8,16,256]{2,1,0:T(8,128)(2,1)S(1)} %get-tuple-element.4.column, bf16[16,32,128]{2,1,0:T(8,128)(2,1)S(1)} %get-tuple-element.5.pair), custom_call_target="tpu_custom_call" | custom-call | tf_op jit(solution)/shard_map/store_results/pallas_call | solution.py:609

commit v7 on v6

--- a/solution.py
+++ b/solution.py
@@ -130,7 +130,8 @@
         (bz_hbm, bz),
     ]
     loads = [pltpu.make_async_copy(a, b, load_sem.at[i]) for i, (a, b) in enumerate(pairs)]
-    loads[0].start()
+    for load in loads[:7]:
+        load.start()
 
     y, xh, core = lax.div(q, 4), lax.rem(lax.div(q, 2), 2), lax.rem(q, 2)
     steps = [(2, 1), (1, 1), (3, 1), (2, 0), (0, 1), (1, 0), (3, 0), (0, 0)]
@@ -171,7 +172,7 @@
         greet(d, there)
     greet(z * 2 + other, q)
 
-    for load in loads[1:]:
+    for load in loads[7:]:
         load.start()
 
     loads[0].wait()
@@ -244,10 +245,7 @@
         pl.semaphore_signal(ready.at[z], inc=1, device_id=line(there), device_id_type=MESH)
         return 0
 
-    def send_far_first(i, _):
-        return send_across(i, 0)
-
-    lax.fori_loop(0, jnp.where(early, 0, QUAD), send_far_first, 0)
+    lax.fori_loop(0, jnp.where(early, 0, QUAD), send_across, 0)
     lax.fori_loop(reach_low, z, send_near, 0)
     lax.fori_loop(0, below, answer_line, 0)
     lax.fori_loop(reach_low, z, answer_line, 0)
@@ -354,7 +352,7 @@
 
         return 0
 
-    lax.fori_loop(QUAD, jnp.where(quad == 2, BLOCK, QUAD), send_far_first, 0)
+    lax.fori_loop(QUAD, jnp.where(quad == 2, BLOCK, QUAD), send_across, 0)
     lax.fori_loop(z + 1, before_high, near_send, 0)
     lax.fori_loop(1, REACH, near_take, 0)
 

time: 28.3 us -> 28.3 us (level)
  no operation moved by 1% of the time
where the time goes in v7:
time: 28.3 us; the launch traced here: 28.1 us
  Pallas kernels  27.5 us (97%)
  between operations  0.64 us (2%)
    pallas_call x1, Pallas kernels, local(): pl.pallas_call(kernel, out_shape=(jax.ShapeDtypeStruct((ROWS, GROUPS, WID...  26.8 us
    pallas_call x1, Pallas kernels, local(): pl.pallas_call(store, out_shape=tuple((jax.ShapeDtypeStruct(r.shape, r.dt...  0.69 us

profile of v7, /device:TPU:249, one launch (start us, length us, event | category | flops | bytes accessed | tf_op | source)
XLA Modules:
  0.0 28.1 jit_solution(14516090527603424506)
XLA Ops:
  0.6 26.8 %column_attention_and_outer_mean.1 = (bf16[8,16,256]{2,1,0:T(8,128)(2,1)S(1)}, bf16[16,32,128]{2,1,0:T(8,128)(2,1)S(1)}) custom-call(bf16[8,16,256]{2,1,0:T(8,128)(2,1)} %x_hbm.1, s32[1,128]{1,0:T(1,128)} %bitcast.12, s32[1,512]{1,0:T(1,128)} %bitcast.10, bf16[256,256]{1,0:T(8,128)(2,1)} %wq_hbm.1, bf16[256,256]{1,0:T(8,128)(2,1)} %wk_hbm.1, ...), custom_call_target="tpu_custom_call" | custom-call | tf_op jit(solution)/shard_map/column_attention_and_outer_mean/pallas_call | solution.py:568
  27.4 0.7 %store_results.1 = (bf16[8,16,256]{2,1,0:T(8,128)(2,1)}, bf16[16,32,128]{2,1,0:T(8,128)(2,1)}) custom-call(bf16[8,16,256]{2,1,0:T(8,128)(2,1)S(1)} %get-tuple-element.4.column, bf16[16,32,128]{2,1,0:T(8,128)(2,1)S(1)} %get-tuple-element.5.pair), custom_call_target="tpu_custom_call" | custom-call | tf_op jit(solution)/shard_map/store_results/pallas_call | solution.py:607

commit v8 on v7

--- a/solution.py
+++ b/solution.py
@@ -199,17 +199,17 @@
     )
     both = keep_rows * keep_residues
     left = ((dot_t(normed, w1[...]) + b1[...]) * both).astype(BF16)
-    right = ((dot_t(normed, w2[...]) + b2[...]) * both).astype(BF16)
+    right = dot_t(normed, jnp.concatenate([w2[...]] * GROUPS, axis=0))
+    right = ((right + jnp.concatenate([b2[...]] * GROUPS, axis=1)) * both).astype(BF16).astype(F32)
 
     factor = iota((FACTORS, 4 * LANES), 0)
     lane = iota((FACTORS, 4 * LANES), 1)
     spread_left = (lax.div(lane, GROUPS) == factor).astype(F32).astype(BF16)
-    spread_right = (lax.rem(lane, FACTORS) == factor).astype(F32).astype(BF16)
     pick_row = iota((ROWS, TOKENS), 0)
     pick_col = iota((ROWS, TOKENS), 1)
     pick = (lax.div(pick_col, GROUPS) == pick_row).astype(F32).astype(BF16)
     left_lanes = jnp.where(lax.rem(col4, GROUPS) == residue, dot(left, spread_left), 0.0)
-    right_lanes = jnp.where(lax.div(col4, FACTORS) == residue, dot(right, spread_right), 0.0)
+    right_lanes = jnp.where(lax.div(col4, FACTORS) == residue, right, 0.0)
     right_rows = dot(pick, right_lanes.astype(BF16))
 
     def fold(rows):

time: 28.3 us -> 28.3 us (level)
  no operation moved by 1% of the time
where the time goes in v8:
time: 28.3 us; the launch traced here: 28.1 us
  Pallas kernels  27.5 us (97%)
  between operations  0.64 us (2%)
    pallas_call x1, Pallas kernels, local(): pl.pallas_call(kernel, out_shape=(jax.ShapeDtypeStruct((ROWS, GROUPS, WID...  26.8 us
    pallas_call x1, Pallas kernels, local(): pl.pallas_call(store, out_shape=tuple((jax.ShapeDtypeStruct(r.shape, r.dt...  0.69 us

profile of v8, /device:TPU:249, one launch (start us, length us, event | category | flops | bytes accessed | tf_op | source)
XLA Modules:
  0.0 28.1 jit_solution(14889444880890589979)
XLA Ops:
  0.6 26.8 %column_attention_and_outer_mean.1 = (bf16[8,16,256]{2,1,0:T(8,128)(2,1)S(1)}, bf16[16,32,128]{2,1,0:T(8,128)(2,1)S(1)}) custom-call(bf16[8,16,256]{2,1,0:T(8,128)(2,1)} %x_hbm.1, s32[1,128]{1,0:T(1,128)} %bitcast.12, s32[1,512]{1,0:T(1,128)} %bitcast.10, bf16[256,256]{1,0:T(8,128)(2,1)} %wq_hbm.1, bf16[256,256]{1,0:T(8,128)(2,1)} %wk_hbm.1, ...), custom_call_target="tpu_custom_call" | custom-call | tf_op jit(solution)/shard_map/column_attention_and_outer_mean/pallas_call | solution.py:568
  27.4 0.7 %store_results.1 = (bf16[8,16,256]{2,1,0:T(8,128)(2,1)}, bf16[16,32,128]{2,1,0:T(8,128)(2,1)}) custom-call(bf16[8,16,256]{2,1,0:T(8,128)(2,1)S(1)} %get-tuple-element.4.column, bf16[16,32,128]{2,1,0:T(8,128)(2,1)S(1)} %get-tuple-element.5.pair), custom_call_target="tpu_custom_call" | custom-call | tf_op jit(solution)/shard_map/store_results/pallas_call | solution.py:607
